TPU v7x, 256 devices: a whole 4x4x8 slice. The times are simulated.
256 devices in a mesh: band: 32 (over x, y, core), sub: 8 (over z).
Axes of the slice: x: 4, y: 4, z: 8, core: 2. Of those that a mesh axis runs over, the one named last changes fastest.
Arguments:
- panels: bfloat16 [32, 8, 32, 256, 256], P('band', 'sub'), may hold values from -0.375 to 0.375
- chain_map: float32 [32, 256, 256], P('band'), as said below
- couplers: bfloat16 [32, 8, 32, 16, 256], P('band', 'sub'), may hold values from -0.375 to 0.375
- anc_band: int32 [8192, 4], P(('band', 'sub')), may hold values from 0 to 31, all different within a row; in each aligned block of 32 rows (0 to 31, 32 to 63, ...) at most 8 rows name the same one
- anc_slot: int32 [8192, 4], P(('band', 'sub')), may hold values from 0 to 31
Outputs:
- front: float32 [32, 256, 256], P('band')
- grads: float32 [32, 8, 32, 16, 256], P('band', 'sub')
Inputs may be any that keep to these rules, and one draw needn't show every extreme that they name: Each row of anc_band lists 4 different bands; among the 32 rows of one device no band is named more than 8 times, a bound that some block reaches. `chain_map`: each band's matrix is a diagonal of entries in (0.5, 0.98) plus small dense off-diagonal entries.
All inputs are finite; a program needn't handle non-finite values.
Results may differ from a plain program's by a relative error of at most 0.0026.
Values may be sent and summed in bfloat16 or wider, within the bound.
A program may use at most 64 MiB of HBM per device.

v0:
```python
import jax
import jax.numpy as jnp
from jax import lax
from jax.sharding import PartitionSpec as P


def shifted(block, axis, distance):
    devices = range(lax.axis_size(axis))
    route = [(i - distance, i) for i in devices if i - distance in devices]
    return lax.ppermute(block, axis, route)


def body(panels, chain_map, couplers, anc_band, anc_slot):
    hi = lax.Precision.HIGHEST
    blocks = panels[0, 0]
    count = blocks.shape[0]
    width = blocks.shape[1]
    nbands = lax.axis_size("band")
    gram = jnp.einsum("jik,jil->kl", blocks, blocks, preferred_element_type=jnp.float32)
    update = lax.psum(gram / (lax.axis_size("sub") * count), "sub")
    matrix = chain_map[0]
    zeros = jnp.zeros((width, width), jnp.float32)

    def apply_map(state):
        return update + jnp.dot(jnp.dot(matrix, state, precision=hi), matrix.T, precision=hi)

    def forward(step, carry):
        incoming = shifted(carry[1], "band", 1)
        return (incoming, apply_map(incoming))

    incoming, _ = lax.fori_loop(0, nbands - 1, forward, (zeros, update))
    coupled = jnp.einsum("jrk,jkl->jrl", couplers[0, 0], blocks, preferred_element_type=jnp.float32)
    adjoint = jnp.einsum("jrk,kl->jrl", coupled, incoming, precision=hi)
    rows_blk = adjoint.shape[1]
    sent = adjoint.astype(jnp.bfloat16).reshape(count, rows_blk * width)
    listed = anc_band.shape[1]
    capacity = max(2, (2 * count * listed + nbands - 1) // nbands)
    flat_dest = anc_band.reshape(-1)
    flat_slot = anc_slot.reshape(-1)
    dest_hot = (flat_dest[:, None] == jnp.arange(nbands, dtype=jnp.int32)[None, :]).astype(
        jnp.int32
    )
    before = jnp.cumsum(dest_hot, axis=0) - dest_hot
    position = flat_dest * capacity + jnp.sum(before * dest_hot, axis=1)
    matches = position[None, :] == jnp.arange(nbands * capacity, dtype=jnp.int32)[:, None]
    source = jnp.arange(count * listed, dtype=jnp.int32) // listed
    source_hot = (source[:, None] == jnp.arange(count, dtype=jnp.int32)[None, :]).astype(
        jnp.bfloat16
    )
    select = jnp.dot(
        matches.astype(jnp.bfloat16), source_hot, preferred_element_type=jnp.float32
    ).astype(jnp.bfloat16)
    outgoing = jnp.dot(select, sent, preferred_element_type=jnp.float32).astype(jnp.bfloat16)
    outgoing = outgoing.reshape(nbands, capacity, rows_blk, width)
    targets = jnp.sum(matches.astype(jnp.int32) * (flat_slot + 1)[None, :], axis=1) - 1
    targets = targets.reshape(nbands, capacity)
    arrived, arrived_slot = (
        lax.all_to_all(outgoing, "band", split_axis=0, concat_axis=0, tiled=True),
        lax.all_to_all(targets, "band", split_axis=0, concat_axis=0, tiled=True),
    )
    landing = (
        arrived_slot.reshape(-1)[None, :] == jnp.arange(count, dtype=jnp.int32)[:, None]
    ).astype(jnp.bfloat16)
    received = jnp.dot(
        landing,
        arrived.reshape(nbands * capacity, rows_blk * width),
        preferred_element_type=jnp.float32,
    )
    grads = adjoint + received.reshape(count, rows_blk, width)
    return (incoming[None], grads[None, None])


def solution(mesh):
    in_specs = (
        P("band", "sub", None, None, None),
        P("band", None, None),
        P("band", "sub", None, None, None),
        P(("band", "sub"), None),
        P(("band", "sub"), None),
    )
    out_specs = (P("band", None, None), P("band", "sub", None, None, None))
    return jax.shard_map(body, mesh=mesh, in_specs=in_specs, out_specs=out_specs, check_vma=False)
```

profile of v0, /device:TPU:1, one launch (start us, length us, event | category | flops | bytes accessed | tf_op | source)
XLA Modules:
  0.0 502.0 jit_solution(375942193251244517)
XLA Ops:
  7.2 5.5 %fusion.7 = f32[256,256]{1,0:T(8,128)} fusion(bf16[1,1,32,256,256]{4,3,2,1,0:T(8,128)(2,1)} %param.7), kind=kOutput, calls=%fused_computation.7 | convolution fusion | flops 1073807360 | bytes 4456448 | tf_op jit(solution)/shard_map/jik,jil->kl/dot_general | solution.py:19
  14.5 8.6 %all-to-all-start = ((s32[32,1,8]{2,1,0:T(1,128)}), s32[32,1,8]{2,1,0:T(1,128)S(1)}, u32[]{:S(2)}, u32[]{:S(2)}) async-start(s32[32,1,8]{2,1,0:T(1,128)} %bitcast.6), calls=%async_computation | async-start | bytes 32768 | tf_op jit(solution)/shard_map/all_to_all | solution.py:59
  26.0 58.7 %all-reduce.2.cloned.1.call-done = f32[256,256]{1,0:T(8,128)} async-done(((f32[256,256]{1,0:T(8,128)}), f32[256,256]{1,0:T(8,128)}) %all-reduce.2.cloned.1.call-update) | async-done | bytes 262160 | tf_op jit(solution)/shard_map/psum | solution.py:20
  85.6 331.1 %while.12 = (s32[]{:T(128)}, f32[256,256]{1,0:T(8,128)}, f32[256,256]{1,0:T(8,128)S(1)}, f32[256,256]{1,0:T(8,128)S(1)}, f32[256,256]{1,0:T(8,128)}, /*index=5*/s32[]{:T(128)}) while((s32[]{:T(128)}, f32[256,256]{1,0:T(8,128)}, f32[256,256]{1,0:T(8,128)S(1)}, f32[256,256]{1,0:T(8,128)S(1)}, f32[256,256]{1,0:T(8,128)}, ...), condition=%wide.region_2.0_spmd, body=%wide.region_1.0_spmd.sunk | while | flops 402718720 | bytes 3932297 | solution.py:31
  85.6 8.2 %collective-permute-start = (f32[256,256]{1,0:T(8,128)S(1)}, f32[256,256]{1,0:T(8,128)S(1)}, u32[]{:S(2)}, u32[]{:S(2)}) collective-permute-start(f32[256,256]{1,0:T(8,128)S(1)} %get-tuple-element.80), channel_id=1, source_target_pairs={{0,8},{8,16},{16,24},{24,32},{32,40},{40,48},{48,56},{56,64},{64,7... | collective-permute-start | bytes 786440 | tf_op jit(solution)/shard_map/while/body/eval_jaxpr/ppermute | solution.py:10
  98.9 4.4 collective-permute-start
  108.4 4.4 collective-permute-start
  117.8 4.4 collective-permute-start
  127.3 4.4 collective-permute-start
  136.8 4.4 collective-permute-start
  146.2 4.4 collective-permute-start
  155.7 4.4 collective-permute-start
  174.7 4.4 collective-permute-start
  203.1 4.4 collective-permute-start
  231.5 6.4 %collective-permute-start = (f32[256,256]{1,0:T(8,128)S(1)}, f32[256,256]{1,0:T(8,128)S(1)}, u32[]{:S(2)}, u32[]{:S(2)}) collective-permute-start(f32[256,256]{1,0:T(8,128)S(1)} %get-tuple-element.80), channel_id=1, source_target_pairs={{0,8},{8,16},{16,24},{24,32},{32,40},{40,48},{48,56},{56,64},{64,7... | collective-permute-start | bytes 786440 | tf_op jit(solution)/shard_map/while/body/eval_jaxpr/ppermute | solution.py:10
  243.0 6.5 %collective-permute-start = (f32[256,256]{1,0:T(8,128)S(1)}, f32[256,256]{1,0:T(8,128)S(1)}, u32[]{:S(2)}, u32[]{:S(2)}) collective-permute-start(f32[256,256]{1,0:T(8,128)S(1)} %get-tuple-element.80), channel_id=1, source_target_pairs={{0,8},{8,16},{16,24},{24,32},{32,40},{40,48},{48,56},{56,64},{64,7... | collective-permute-start | bytes 786440 | tf_op jit(solution)/shard_map/while/body/eval_jaxpr/ppermute | solution.py:10
  254.6 6.5 %collective-permute-start = (f32[256,256]{1,0:T(8,128)S(1)}, f32[256,256]{1,0:T(8,128)S(1)}, u32[]{:S(2)}, u32[]{:S(2)}) collective-permute-start(f32[256,256]{1,0:T(8,128)S(1)} %get-tuple-element.80), channel_id=1, source_target_pairs={{0,8},{8,16},{16,24},{24,32},{32,40},{40,48},{48,56},{56,64},{64,7... | collective-permute-start | bytes 786440 | tf_op jit(solution)/shard_map/while/body/eval_jaxpr/ppermute | solution.py:10
  266.2 6.5 %collective-permute-start = (f32[256,256]{1,0:T(8,128)S(1)}, f32[256,256]{1,0:T(8,128)S(1)}, u32[]{:S(2)}, u32[]{:S(2)}) collective-permute-start(f32[256,256]{1,0:T(8,128)S(1)} %get-tuple-element.80), channel_id=1, source_target_pairs={{0,8},{8,16},{16,24},{24,32},{32,40},{40,48},{48,56},{56,64},{64,7... | collective-permute-start | bytes 786440 | tf_op jit(solution)/shard_map/while/body/eval_jaxpr/ppermute | solution.py:10
  277.8 6.5 %collective-permute-start = (f32[256,256]{1,0:T(8,128)S(1)}, f32[256,256]{1,0:T(8,128)S(1)}, u32[]{:S(2)}, u32[]{:S(2)}) collective-permute-start(f32[256,256]{1,0:T(8,128)S(1)} %get-tuple-element.80), channel_id=1, source_target_pairs={{0,8},{8,16},{16,24},{24,32},{32,40},{40,48},{48,56},{56,64},{64,7... | collective-permute-start | bytes 786440 | tf_op jit(solution)/shard_map/while/body/eval_jaxpr/ppermute | solution.py:10
  289.3 6.5 %collective-permute-start = (f32[256,256]{1,0:T(8,128)S(1)}, f32[256,256]{1,0:T(8,128)S(1)}, u32[]{:S(2)}, u32[]{:S(2)}) collective-permute-start(f32[256,256]{1,0:T(8,128)S(1)} %get-tuple-element.80), channel_id=1, source_target_pairs={{0,8},{8,16},{16,24},{24,32},{32,40},{40,48},{48,56},{56,64},{64,7... | collective-permute-start | bytes 786440 | tf_op jit(solution)/shard_map/while/body/eval_jaxpr/ppermute | solution.py:10
  300.9 6.5 %collective-permute-start = (f32[256,256]{1,0:T(8,128)S(1)}, f32[256,256]{1,0:T(8,128)S(1)}, u32[]{:S(2)}, u32[]{:S(2)}) collective-permute-start(f32[256,256]{1,0:T(8,128)S(1)} %get-tuple-element.80), channel_id=1, source_target_pairs={{0,8},{8,16},{16,24},{24,32},{32,40},{40,48},{48,56},{56,64},{64,7... | collective-permute-start | bytes 786440 | tf_op jit(solution)/shard_map/while/body/eval_jaxpr/ppermute | solution.py:10
  312.5 6.5 %collective-permute-start = (f32[256,256]{1,0:T(8,128)S(1)}, f32[256,256]{1,0:T(8,128)S(1)}, u32[]{:S(2)}, u32[]{:S(2)}) collective-permute-start(f32[256,256]{1,0:T(8,128)S(1)} %get-tuple-element.80), channel_id=1, source_target_pairs={{0,8},{8,16},{16,24},{24,32},{32,40},{40,48},{48,56},{56,64},{64,7... | collective-permute-start | bytes 786440 | tf_op jit(solution)/shard_map/while/body/eval_jaxpr/ppermute | solution.py:10
  324.1 6.5 %collective-permute-start = (f32[256,256]{1,0:T(8,128)S(1)}, f32[256,256]{1,0:T(8,128)S(1)}, u32[]{:S(2)}, u32[]{:S(2)}) collective-permute-start(f32[256,256]{1,0:T(8,128)S(1)} %get-tuple-element.80), channel_id=1, source_target_pairs={{0,8},{8,16},{16,24},{24,32},{32,40},{40,48},{48,56},{56,64},{64,7... | collective-permute-start | bytes 786440 | tf_op jit(solution)/shard_map/while/body/eval_jaxpr/ppermute | solution.py:10
  335.6 6.5 %collective-permute-start = (f32[256,256]{1,0:T(8,128)S(1)}, f32[256,256]{1,0:T(8,128)S(1)}, u32[]{:S(2)}, u32[]{:S(2)}) collective-permute-start(f32[256,256]{1,0:T(8,128)S(1)} %get-tuple-element.80), channel_id=1, source_target_pairs={{0,8},{8,16},{16,24},{24,32},{32,40},{40,48},{48,56},{56,64},{64,7... | collective-permute-start | bytes 786440 | tf_op jit(solution)/shard_map/while/body/eval_jaxpr/ppermute | solution.py:10
  347.2 6.5 %collective-permute-start = (f32[256,256]{1,0:T(8,128)S(1)}, f32[256,256]{1,0:T(8,128)S(1)}, u32[]{:S(2)}, u32[]{:S(2)}) collective-permute-start(f32[256,256]{1,0:T(8,128)S(1)} %get-tuple-element.80), channel_id=1, source_target_pairs={{0,8},{8,16},{16,24},{24,32},{32,40},{40,48},{48,56},{56,64},{64,7... | collective-permute-start | bytes 786440 | tf_op jit(solution)/shard_map/while/body/eval_jaxpr/ppermute | solution.py:10
  358.8 6.5 %collective-permute-start = (f32[256,256]{1,0:T(8,128)S(1)}, f32[256,256]{1,0:T(8,128)S(1)}, u32[]{:S(2)}, u32[]{:S(2)}) collective-permute-start(f32[256,256]{1,0:T(8,128)S(1)} %get-tuple-element.80), channel_id=1, source_target_pairs={{0,8},{8,16},{16,24},{24,32},{32,40},{40,48},{48,56},{56,64},{64,7... | collective-permute-start | bytes 786440 | tf_op jit(solution)/shard_map/while/body/eval_jaxpr/ppermute | solution.py:10
  370.4 6.5 %collective-permute-start = (f32[256,256]{1,0:T(8,128)S(1)}, f32[256,256]{1,0:T(8,128)S(1)}, u32[]{:S(2)}, u32[]{:S(2)}) collective-permute-start(f32[256,256]{1,0:T(8,128)S(1)} %get-tuple-element.80), channel_id=1, source_target_pairs={{0,8},{8,16},{16,24},{24,32},{32,40},{40,48},{48,56},{56,64},{64,7... | collective-permute-start | bytes 786440 | tf_op jit(solution)/shard_map/while/body/eval_jaxpr/ppermute | solution.py:10
  382.0 6.5 %collective-permute-start = (f32[256,256]{1,0:T(8,128)S(1)}, f32[256,256]{1,0:T(8,128)S(1)}, u32[]{:S(2)}, u32[]{:S(2)}) collective-permute-start(f32[256,256]{1,0:T(8,128)S(1)} %get-tuple-element.80), channel_id=1, source_target_pairs={{0,8},{8,16},{16,24},{24,32},{32,40},{40,48},{48,56},{56,64},{64,7... | collective-permute-start | bytes 786440 | tf_op jit(solution)/shard_map/while/body/eval_jaxpr/ppermute | solution.py:10
  393.5 6.5 %collective-permute-start = (f32[256,256]{1,0:T(8,128)S(1)}, f32[256,256]{1,0:T(8,128)S(1)}, u32[]{:S(2)}, u32[]{:S(2)}) collective-permute-start(f32[256,256]{1,0:T(8,128)S(1)} %get-tuple-element.80), channel_id=1, source_target_pairs={{0,8},{8,16},{16,24},{24,32},{32,40},{40,48},{48,56},{56,64},{64,7... | collective-permute-start | bytes 786440 | tf_op jit(solution)/shard_map/while/body/eval_jaxpr/ppermute | solution.py:10
  405.1 6.5 %collective-permute-start = (f32[256,256]{1,0:T(8,128)S(1)}, f32[256,256]{1,0:T(8,128)S(1)}, u32[]{:S(2)}, u32[]{:S(2)}) collective-permute-start(f32[256,256]{1,0:T(8,128)S(1)} %get-tuple-element.80), channel_id=1, source_target_pairs={{0,8},{8,16},{16,24},{24,32},{32,40},{40,48},{48,56},{56,64},{64,7... | collective-permute-start | bytes 786440 | tf_op jit(solution)/shard_map/while/body/eval_jaxpr/ppermute | solution.py:10
  421.3 37.5 %all-to-all-start.1 = ((bf16[32,8,16,256]{3,2,1,0:T(8,128)(2,1)}), bf16[32,8,16,256]{3,2,1,0:T(8,128)(2,1)S(1)}, u32[]{:S(2)}, u32[]{:S(2)}) async-start(bf16[32,8,16,256]{3,2,1,0:T(8,128)(2,1)} %copy.28), calls=%async_computation.1 | async-start | bytes 4194304 | tf_op jit(solution)/shard_map/all_to_all | solution.py:58
  460.1 27.0 %all-to-all-done.1 = bf16[32,8,16,256]{3,2,1,0:T(8,128)(2,1)S(1)} async-done(((bf16[32,8,16,256]{3,2,1,0:T(8,128)(2,1)}), bf16[32,8,16,256]{3,2,1,0:T(8,128)(2,1)S(1)}, u32[]{:S(2)}, u32[]{:S(2)}) %all-to-all-start.1) | async-done | bytes 2097184 | tf_op jit(solution)/shard_map/all_to_all | solution.py:58
  (200 shorter events, 197.5 us)
Async XLA Ops:
  7.2 77.5 %all-reduce.2.cloned.1.call-start = ((), (), s32[]{:S(2)}) async-start(), calls=%async_computation.2 | async-start | bytes 524288 | tf_op jit(solution)/shard_map/psum | solution.py:20
  14.5 406.9 %all-to-all-start = ((s32[32,1,8]{2,1,0:T(1,128)}), s32[32,1,8]{2,1,0:T(1,128)S(1)}, u32[]{:S(2)}, u32[]{:S(2)}) async-start(s32[32,1,8]{2,1,0:T(1,128)} %bitcast.6), calls=%async_computation | async-start | bytes 32768 | tf_op jit(solution)/shard_map/all_to_all | solution.py:59
  85.6 11.5 %collective-permute-start = (f32[256,256]{1,0:T(8,128)S(1)}, f32[256,256]{1,0:T(8,128)S(1)}, u32[]{:S(2)}, u32[]{:S(2)}) collective-permute-start(f32[256,256]{1,0:T(8,128)S(1)} %get-tuple-element.80), channel_id=1, source_target_pairs={{0,8},{8,16},{16,24},{24,32},{32,40},{40,48},{48,56},{56,64},{64,7... | collective-permute-start | bytes 786440 | tf_op jit(solution)/shard_map/while/body/eval_jaxpr/ppermute | solution.py:10
  98.9 7.7 %collective-permute-start = (f32[256,256]{1,0:T(8,128)S(1)}, f32[256,256]{1,0:T(8,128)S(1)}, u32[]{:S(2)}, u32[]{:S(2)}) collective-permute-start(f32[256,256]{1,0:T(8,128)S(1)} %get-tuple-element.80), channel_id=1, source_target_pairs={{0,8},{8,16},{16,24},{24,32},{32,40},{40,48},{48,56},{56,64},{64,7... | collective-permute-start | bytes 786440 | tf_op jit(solution)/shard_map/while/body/eval_jaxpr/ppermute | solution.py:10
  108.4 7.7 %collective-permute-start = (f32[256,256]{1,0:T(8,128)S(1)}, f32[256,256]{1,0:T(8,128)S(1)}, u32[]{:S(2)}, u32[]{:S(2)}) collective-permute-start(f32[256,256]{1,0:T(8,128)S(1)} %get-tuple-element.80), channel_id=1, source_target_pairs={{0,8},{8,16},{16,24},{24,32},{32,40},{40,48},{48,56},{56,64},{64,7... | collective-permute-start | bytes 786440 | tf_op jit(solution)/shard_map/while/body/eval_jaxpr/ppermute | solution.py:10
  117.8 7.7 %collective-permute-start = (f32[256,256]{1,0:T(8,128)S(1)}, f32[256,256]{1,0:T(8,128)S(1)}, u32[]{:S(2)}, u32[]{:S(2)}) collective-permute-start(f32[256,256]{1,0:T(8,128)S(1)} %get-tuple-element.80), channel_id=1, source_target_pairs={{0,8},{8,16},{16,24},{24,32},{32,40},{40,48},{48,56},{56,64},{64,7... | collective-permute-start | bytes 786440 | tf_op jit(solution)/shard_map/while/body/eval_jaxpr/ppermute | solution.py:10
  127.3 7.7 %collective-permute-start = (f32[256,256]{1,0:T(8,128)S(1)}, f32[256,256]{1,0:T(8,128)S(1)}, u32[]{:S(2)}, u32[]{:S(2)}) collective-permute-start(f32[256,256]{1,0:T(8,128)S(1)} %get-tuple-element.80), channel_id=1, source_target_pairs={{0,8},{8,16},{16,24},{24,32},{32,40},{40,48},{48,56},{56,64},{64,7... | collective-permute-start | bytes 786440 | tf_op jit(solution)/shard_map/while/body/eval_jaxpr/ppermute | solution.py:10
  136.8 7.7 %collective-permute-start = (f32[256,256]{1,0:T(8,128)S(1)}, f32[256,256]{1,0:T(8,128)S(1)}, u32[]{:S(2)}, u32[]{:S(2)}) collective-permute-start(f32[256,256]{1,0:T(8,128)S(1)} %get-tuple-element.80), channel_id=1, source_target_pairs={{0,8},{8,16},{16,24},{24,32},{32,40},{40,48},{48,56},{56,64},{64,7... | collective-permute-start | bytes 786440 | tf_op jit(solution)/shard_map/while/body/eval_jaxpr/ppermute | solution.py:10
  146.2 7.7 %collective-permute-start = (f32[256,256]{1,0:T(8,128)S(1)}, f32[256,256]{1,0:T(8,128)S(1)}, u32[]{:S(2)}, u32[]{:S(2)}) collective-permute-start(f32[256,256]{1,0:T(8,128)S(1)} %get-tuple-element.80), channel_id=1, source_target_pairs={{0,8},{8,16},{16,24},{24,32},{32,40},{40,48},{48,56},{56,64},{64,7... | collective-permute-start | bytes 786440 | tf_op jit(solution)/shard_map/while/body/eval_jaxpr/ppermute | solution.py:10
  165.2 7.7 %collective-permute-start = (f32[256,256]{1,0:T(8,128)S(1)}, f32[256,256]{1,0:T(8,128)S(1)}, u32[]{:S(2)}, u32[]{:S(2)}) collective-permute-start(f32[256,256]{1,0:T(8,128)S(1)} %get-tuple-element.80), channel_id=1, source_target_pairs={{0,8},{8,16},{16,24},{24,32},{32,40},{40,48},{48,56},{56,64},{64,7... | collective-permute-start | bytes 786440 | tf_op jit(solution)/shard_map/while/body/eval_jaxpr/ppermute | solution.py:10
  174.7 7.7 %collective-permute-start = (f32[256,256]{1,0:T(8,128)S(1)}, f32[256,256]{1,0:T(8,128)S(1)}, u32[]{:S(2)}, u32[]{:S(2)}) collective-permute-start(f32[256,256]{1,0:T(8,128)S(1)} %get-tuple-element.80), channel_id=1, source_target_pairs={{0,8},{8,16},{16,24},{24,32},{32,40},{40,48},{48,56},{56,64},{64,7... | collective-permute-start | bytes 786440 | tf_op jit(solution)/shard_map/while/body/eval_jaxpr/ppermute | solution.py:10
  184.1 7.7 %collective-permute-start = (f32[256,256]{1,0:T(8,128)S(1)}, f32[256,256]{1,0:T(8,128)S(1)}, u32[]{:S(2)}, u32[]{:S(2)}) collective-permute-start(f32[256,256]{1,0:T(8,128)S(1)} %get-tuple-element.80), channel_id=1, source_target_pairs={{0,8},{8,16},{16,24},{24,32},{32,40},{40,48},{48,56},{56,64},{64,7... | collective-permute-start | bytes 786440 | tf_op jit(solution)/shard_map/while/body/eval_jaxpr/ppermute | solution.py:10
  193.6 7.7 %collective-permute-start = (f32[256,256]{1,0:T(8,128)S(1)}, f32[256,256]{1,0:T(8,128)S(1)}, u32[]{:S(2)}, u32[]{:S(2)}) collective-permute-start(f32[256,256]{1,0:T(8,128)S(1)} %get-tuple-element.80), channel_id=1, source_target_pairs={{0,8},{8,16},{16,24},{24,32},{32,40},{40,48},{48,56},{56,64},{64,7... | collective-permute-start | bytes 786440 | tf_op jit(solution)/shard_map/while/body/eval_jaxpr/ppermute | solution.py:10
  203.1 7.7 %collective-permute-start = (f32[256,256]{1,0:T(8,128)S(1)}, f32[256,256]{1,0:T(8,128)S(1)}, u32[]{:S(2)}, u32[]{:S(2)}) collective-permute-start(f32[256,256]{1,0:T(8,128)S(1)} %get-tuple-element.80), channel_id=1, source_target_pairs={{0,8},{8,16},{16,24},{24,32},{32,40},{40,48},{48,56},{56,64},{64,7... | collective-permute-start | bytes 786440 | tf_op jit(solution)/shard_map/while/body/eval_jaxpr/ppermute | solution.py:10
  212.5 7.7 %collective-permute-start = (f32[256,256]{1,0:T(8,128)S(1)}, f32[256,256]{1,0:T(8,128)S(1)}, u32[]{:S(2)}, u32[]{:S(2)}) collective-permute-start(f32[256,256]{1,0:T(8,128)S(1)} %get-tuple-element.80), channel_id=1, source_target_pairs={{0,8},{8,16},{16,24},{24,32},{32,40},{40,48},{48,56},{56,64},{64,7... | collective-permute-start | bytes 786440 | tf_op jit(solution)/shard_map/while/body/eval_jaxpr/ppermute | solution.py:10
  231.5 9.7 %collective-permute-start = (f32[256,256]{1,0:T(8,128)S(1)}, f32[256,256]{1,0:T(8,128)S(1)}, u32[]{:S(2)}, u32[]{:S(2)}) collective-permute-start(f32[256,256]{1,0:T(8,128)S(1)} %get-tuple-element.80), channel_id=1, source_target_pairs={{0,8},{8,16},{16,24},{24,32},{32,40},{40,48},{48,56},{56,64},{64,7... | collective-permute-start | bytes 786440 | tf_op jit(solution)/shard_map/while/body/eval_jaxpr/ppermute | solution.py:10
  243.0 9.8 %collective-permute-start = (f32[256,256]{1,0:T(8,128)S(1)}, f32[256,256]{1,0:T(8,128)S(1)}, u32[]{:S(2)}, u32[]{:S(2)}) collective-permute-start(f32[256,256]{1,0:T(8,128)S(1)} %get-tuple-element.80), channel_id=1, source_target_pairs={{0,8},{8,16},{16,24},{24,32},{32,40},{40,48},{48,56},{56,64},{64,7... | collective-permute-start | bytes 786440 | tf_op jit(solution)/shard_map/while/body/eval_jaxpr/ppermute | solution.py:10
  254.6 9.8 %collective-permute-start = (f32[256,256]{1,0:T(8,128)S(1)}, f32[256,256]{1,0:T(8,128)S(1)}, u32[]{:S(2)}, u32[]{:S(2)}) collective-permute-start(f32[256,256]{1,0:T(8,128)S(1)} %get-tuple-element.80), channel_id=1, source_target_pairs={{0,8},{8,16},{16,24},{24,32},{32,40},{40,48},{48,56},{56,64},{64,7... | collective-permute-start | bytes 786440 | tf_op jit(solution)/shard_map/while/body/eval_jaxpr/ppermute | solution.py:10
  266.2 9.8 %collective-permute-start = (f32[256,256]{1,0:T(8,128)S(1)}, f32[256,256]{1,0:T(8,128)S(1)}, u32[]{:S(2)}, u32[]{:S(2)}) collective-permute-start(f32[256,256]{1,0:T(8,128)S(1)} %get-tuple-element.80), channel_id=1, source_target_pairs={{0,8},{8,16},{16,24},{24,32},{32,40},{40,48},{48,56},{56,64},{64,7... | collective-permute-start | bytes 786440 | tf_op jit(solution)/shard_map/while/body/eval_jaxpr/ppermute | solution.py:10
  277.8 9.8 %collective-permute-start = (f32[256,256]{1,0:T(8,128)S(1)}, f32[256,256]{1,0:T(8,128)S(1)}, u32[]{:S(2)}, u32[]{:S(2)}) collective-permute-start(f32[256,256]{1,0:T(8,128)S(1)} %get-tuple-element.80), channel_id=1, source_target_pairs={{0,8},{8,16},{16,24},{24,32},{32,40},{40,48},{48,56},{56,64},{64,7... | collective-permute-start | bytes 786440 | tf_op jit(solution)/shard_map/while/body/eval_jaxpr/ppermute | solution.py:10
  289.3 9.8 %collective-permute-start = (f32[256,256]{1,0:T(8,128)S(1)}, f32[256,256]{1,0:T(8,128)S(1)}, u32[]{:S(2)}, u32[]{:S(2)}) collective-permute-start(f32[256,256]{1,0:T(8,128)S(1)} %get-tuple-element.80), channel_id=1, source_target_pairs={{0,8},{8,16},{16,24},{24,32},{32,40},{40,48},{48,56},{56,64},{64,7... | collective-permute-start | bytes 786440 | tf_op jit(solution)/shard_map/while/body/eval_jaxpr/ppermute | solution.py:10
  300.9 9.8 %collective-permute-start = (f32[256,256]{1,0:T(8,128)S(1)}, f32[256,256]{1,0:T(8,128)S(1)}, u32[]{:S(2)}, u32[]{:S(2)}) collective-permute-start(f32[256,256]{1,0:T(8,128)S(1)} %get-tuple-element.80), channel_id=1, source_target_pairs={{0,8},{8,16},{16,24},{24,32},{32,40},{40,48},{48,56},{56,64},{64,7... | collective-permute-start | bytes 786440 | tf_op jit(solution)/shard_map/while/body/eval_jaxpr/ppermute | solution.py:10
  312.5 9.8 %collective-permute-start = (f32[256,256]{1,0:T(8,128)S(1)}, f32[256,256]{1,0:T(8,128)S(1)}, u32[]{:S(2)}, u32[]{:S(2)}) collective-permute-start(f32[256,256]{1,0:T(8,128)S(1)} %get-tuple-element.80), channel_id=1, source_target_pairs={{0,8},{8,16},{16,24},{24,32},{32,40},{40,48},{48,56},{56,64},{64,7... | collective-permute-start | bytes 786440 | tf_op jit(solution)/shard_map/while/body/eval_jaxpr/ppermute | solution.py:10
  324.1 9.8 %collective-permute-start = (f32[256,256]{1,0:T(8,128)S(1)}, f32[256,256]{1,0:T(8,128)S(1)}, u32[]{:S(2)}, u32[]{:S(2)}) collective-permute-start(f32[256,256]{1,0:T(8,128)S(1)} %get-tuple-element.80), channel_id=1, source_target_pairs={{0,8},{8,16},{16,24},{24,32},{32,40},{40,48},{48,56},{56,64},{64,7... | collective-permute-start | bytes 786440 | tf_op jit(solution)/shard_map/while/body/eval_jaxpr/ppermute | solution.py:10
  335.6 9.8 %collective-permute-start = (f32[256,256]{1,0:T(8,128)S(1)}, f32[256,256]{1,0:T(8,128)S(1)}, u32[]{:S(2)}, u32[]{:S(2)}) collective-permute-start(f32[256,256]{1,0:T(8,128)S(1)} %get-tuple-element.80), channel_id=1, source_target_pairs={{0,8},{8,16},{16,24},{24,32},{32,40},{40,48},{48,56},{56,64},{64,7... | collective-permute-start | bytes 786440 | tf_op jit(solution)/shard_map/while/body/eval_jaxpr/ppermute | solution.py:10
  347.2 9.8 %collective-permute-start = (f32[256,256]{1,0:T(8,128)S(1)}, f32[256,256]{1,0:T(8,128)S(1)}, u32[]{:S(2)}, u32[]{:S(2)}) collective-permute-start(f32[256,256]{1,0:T(8,128)S(1)} %get-tuple-element.80), channel_id=1, source_target_pairs={{0,8},{8,16},{16,24},{24,32},{32,40},{40,48},{48,56},{56,64},{64,7... | collective-permute-start | bytes 786440 | tf_op jit(solution)/shard_map/while/body/eval_jaxpr/ppermute | solution.py:10
  358.8 9.8 %collective-permute-start = (f32[256,256]{1,0:T(8,128)S(1)}, f32[256,256]{1,0:T(8,128)S(1)}, u32[]{:S(2)}, u32[]{:S(2)}) collective-permute-start(f32[256,256]{1,0:T(8,128)S(1)} %get-tuple-element.80), channel_id=1, source_target_pairs={{0,8},{8,16},{16,24},{24,32},{32,40},{40,48},{48,56},{56,64},{64,7... | collective-permute-start | bytes 786440 | tf_op jit(solution)/shard_map/while/body/eval_jaxpr/ppermute | solution.py:10
  370.4 9.8 %collective-permute-start = (f32[256,256]{1,0:T(8,128)S(1)}, f32[256,256]{1,0:T(8,128)S(1)}, u32[]{:S(2)}, u32[]{:S(2)}) collective-permute-start(f32[256,256]{1,0:T(8,128)S(1)} %get-tuple-element.80), channel_id=1, source_target_pairs={{0,8},{8,16},{16,24},{24,32},{32,40},{40,48},{48,56},{56,64},{64,7... | collective-permute-start | bytes 786440 | tf_op jit(solution)/shard_map/while/body/eval_jaxpr/ppermute | solution.py:10
  382.0 9.8 %collective-permute-start = (f32[256,256]{1,0:T(8,128)S(1)}, f32[256,256]{1,0:T(8,128)S(1)}, u32[]{:S(2)}, u32[]{:S(2)}) collective-permute-start(f32[256,256]{1,0:T(8,128)S(1)} %get-tuple-element.80), channel_id=1, source_target_pairs={{0,8},{8,16},{16,24},{24,32},{32,40},{40,48},{48,56},{56,64},{64,7... | collective-permute-start | bytes 786440 | tf_op jit(solution)/shard_map/while/body/eval_jaxpr/ppermute | solution.py:10
  393.5 9.8 %collective-permute-start = (f32[256,256]{1,0:T(8,128)S(1)}, f32[256,256]{1,0:T(8,128)S(1)}, u32[]{:S(2)}, u32[]{:S(2)}) collective-permute-start(f32[256,256]{1,0:T(8,128)S(1)} %get-tuple-element.80), channel_id=1, source_target_pairs={{0,8},{8,16},{16,24},{24,32},{32,40},{40,48},{48,56},{56,64},{64,7... | collective-permute-start | bytes 786440 | tf_op jit(solution)/shard_map/while/body/eval_jaxpr/ppermute | solution.py:10
  405.1 9.8 %collective-permute-start = (f32[256,256]{1,0:T(8,128)S(1)}, f32[256,256]{1,0:T(8,128)S(1)}, u32[]{:S(2)}, u32[]{:S(2)}) collective-permute-start(f32[256,256]{1,0:T(8,128)S(1)} %get-tuple-element.80), channel_id=1, source_target_pairs={{0,8},{8,16},{16,24},{24,32},{32,40},{40,48},{48,56},{56,64},{64,7... | collective-permute-start | bytes 786440 | tf_op jit(solution)/shard_map/while/body/eval_jaxpr/ppermute | solution.py:10
  421.3 65.8 %all-to-all-start.1 = ((bf16[32,8,16,256]{3,2,1,0:T(8,128)(2,1)}), bf16[32,8,16,256]{3,2,1,0:T(8,128)(2,1)S(1)}, u32[]{:S(2)}, u32[]{:S(2)}) async-start(bf16[32,8,16,256]{3,2,1,0:T(8,128)(2,1)} %copy.28), calls=%async_computation.1 | async-start | bytes 4194304 | tf_op jit(solution)/shard_map/all_to_all | solution.py:58
  (38 other events, 161.9 us)
Sparse Core Ops, SparseCore 0:
  12.9 71.7 all-reduce.1
where the time goes:
time: 505 us; the launch traced here: 502 us
  starting transfers between devices  220 us (44%)
  waiting for transfers between devices  188 us (37%)
  matrix products  65.4 us (13%)
  between operations  14.2 us (3%)
  local copies, waits for them, and re-layouts  11.1 us (2%)
    ppermute x31, starting transfers between devices, shifted(): return lax.ppermute(block, axis, route)  174 us
    ppermute x31, waiting for transfers between devices, shifted(): return lax.ppermute(block, axis, route)  102 us
    psum x1, waiting for transfers between devices, body(): update = lax.psum(gram / (lax.axis_size('sub') * count), 'sub')  58.7 us
    dot_general x31, matrix products, apply_map(): jnp.dot(jnp.dot(matrix, state, precision=hi), matrix.T, precision=hi)  42.1 us
    all_to_all x1, starting transfers between devices, body(): lax.all_to_all(outgoing, 'band', split_axis=0, concat_axis=0, tiled=True)  37.5 us
    all_to_all x1, waiting for transfers between devices, body(): lax.all_to_all(outgoing, 'band', split_axis=0, concat_axis=0, tiled=True)  27 us
    dot_general x31, matrix products, apply_map(): jnp.dot(matrix, state, precision=hi)  11.7 us
  transfers between devices with their start and end apart: 34, of which 33 were waited for; matrix products, arithmetic and copies ran while one was open for 13% of the time, Pallas kernels for 0%

commit v1 on v0

v1 whole, which is shorter than its diff:
```python
import functools

import jax
import jax.numpy as jnp
from jax import lax
from jax.experimental import pallas as pl
from jax.experimental.pallas import tpu as pltpu
from jax.sharding import PartitionSpec as P

MESH = pl.DeviceIdType.MESH
F32, BF16 = jnp.float32, jnp.bfloat16
CHIPS_X, CHIPS_Y = 4, 4
PAD = 16


def split(value):
    high = value.astype(BF16)
    return high, (value - high.astype(F32)).astype(BF16)


def dot(a, b):
    return jnp.dot(a, b, preferred_element_type=F32)


def dot_t(a, b):
    return lax.dot_general(a, b, (((1,), (1,)), ((), ())), preferred_element_type=F32)


def product(a, b):
    ah, al = split(a)
    bh, bl = split(b)
    return dot(ah, bh) + (dot(ah, bl) + dot(al, bh))


def diagonal(width):
    rows = lax.broadcasted_iota(jnp.int32, (width, width), 0)
    return rows == lax.broadcasted_iota(jnp.int32, (width, width), 1)


def pack(value, message):
    width = value.shape[1]
    high = value.astype(BF16)
    rest = jnp.where(diagonal(width), value - high.astype(F32), 0.0)
    message[0:width, :] = high
    rest = jnp.sum(rest, axis=0, keepdims=True)
    message[width : width + PAD, :] = jnp.broadcast_to(rest, (PAD, width)).astype(BF16)


def unpack(message):
    width = message.shape[1]
    rest = message[width : width + PAD, :].astype(F32)[0:1, :]
    return message[0:width, :].astype(F32) + jnp.where(diagonal(width), rest, 0.0)


def kernel(
    nx, ny, nz, ns, nr,
    panels, map_ref, coup_ref, key_ref,
    front_ref, grads_ref,
    pv, gram, rsbuf, upd, upd_other, map_other, abuf, bbuf, vbuf, tbuf,
    tcat, kcat, wcat, ycat, crm, cjm, gacc, ccat, fcat,
    keys0, keys1, x0, x1, o0, o1, rb0, rb1,
    psem, rs_s, rs_r, ag_s, ag_r, c_s, c_r, y_s, y_r, x_s, x_r, k_s, k_r,
    s1_s, s1_r, fw_s, fw_r, s2_s, s2_r,
):
    width = map_ref.shape[0]
    half = width // 2
    slab = width // nz
    band, z = lax.axis_index("band"), lax.axis_index("sub")
    x, y, c = band // (2 * ny), (band // 2) % ny, band % 2

    def at(xx, yy, cc):
        return {"band": (xx * ny + yy) * 2 + cc}

    sibling = at(x, y, 1 - c)
    xpeer = {d: at((x + d) % nx, y, c) for d in range(1, nx)}
    ypeer = {d: at(x, (y + d) % ny, c) for d in range(1, ny)}
    zpeer = {d: {"sub": (z + d) % nz} for d in range(1, nz)}
    peers = [sibling, *xpeer.values(), *ypeer.values(), *zpeer.values()]
    started = []

    def send(src, dst, s, r, target):
        copy = pltpu.make_async_remote_copy(
            src_ref=src, dst_ref=dst, send_sem=s, recv_sem=r, device_id=target, device_id_type=MESH
        )
        copy.start()
        started.append(copy)
        return copy

    barrier = pltpu.get_barrier_semaphore()
    for peer in peers:
        pl.semaphore_signal(barrier, inc=1, device_id=peer, device_id_type=MESH)
    chunks = psem.shape[0]
    per = ns // chunks
    loads = []
    for q in range(chunks):
        rows = pl.ds(q * per * width, per * width)
        loads.append(pltpu.make_async_copy(panels.at[rows], pv.at[rows], psem.at[q]))
        loads[-1].start()

    def work(q):
        loads[q].wait()
        block = pv[q * per * width : (q + 1) * per * width, :]
        part = lax.dot_general(block, block, (((0,), (0,)), ((), ())), preferred_element_type=F32)
        gram[...] = part if q == 0 else gram[...] + part
        for j in range(q * per, (q + 1) * per):
            value = dot(coup_ref[j * nr : (j + 1) * nr, :], pv[j * width : (j + 1) * width, :])
            cjm[j * nr : (j + 1) * nr, :] = value
            for h in range(2):
                crm[h, pl.ds(j, nr, stride=ns), :] = value[:, h * half : (h + 1) * half]

    work(0)
    pl.semaphore_wait(barrier, len(peers))

    maps = send(map_ref, map_other, c_s.at[0], c_r.at[0], sibling)
    keys0[pl.ds(c * nx + x, 1)] = key_ref[...][None]
    keys1[pl.ds(c * ny + y, 1)] = key_ref[...][None]
    kcopies = []
    for d in range(1, nx):
        own = keys0.at[c * nx + x]
        kcopies.append(send(own, own, k_s.at[0, d], k_r.at[0, d], xpeer[d]))
    for d in range(1, ny):
        own = keys1.at[c * ny + y]
        kcopies.append(send(own, own, k_s.at[1, d], k_r.at[1, d], ypeer[d]))
    for q in range(1, chunks // 2):
        work(q)
    maps.wait_recv()
    mine, other = map_ref[...], map_other[...]
    odd = jnp.where(c == 1, mine, other)
    even = jnp.where(c == 1, other, mine)
    identity = diagonal(width).astype(F32)
    pack(product(odd, even), abuf.at[y])
    acopies = [
        send(abuf.at[y], abuf.at[y], y_s.at[0, d], y_r.at[0, d], ypeer[d]) for d in range(1, ny)
    ]
    for q in range(chunks // 2, chunks):
        work(q)

    gram[...] = gram[...] * (1.0 / (nz * ns))
    rcopies = [
        send(gram.at[pl.ds(((z + d) % nz) * slab, slab)], rsbuf.at[d], rs_s.at[d], rs_r.at[d], zpeer[d])
        for d in range(1, nz)
    ]
    for copy in kcopies:
        copy.wait_recv()
    kcopies = [
        send(keys0.at[pl.ds(c * nx, nx)], keys0.at[pl.ds(c * nx, nx)], k_s.at[0, 0], k_r.at[0, 0], sibling),
        send(keys1.at[pl.ds(c * ny, ny)], keys1.at[pl.ds(c * ny, ny)], k_s.at[1, 0], k_r.at[1, 0], sibling),
    ]
    ch, cl = split(jnp.concatenate([crm[0], crm[1]], axis=1))
    ccat[0, :, 0:width], ccat[0, :, width : 2 * width], ccat[0, :, 2 * width :] = ch, ch, cl
    ch, cl = split(cjm[...])
    ccat[1, :, 0:width], ccat[1, :, width : 2 * width], ccat[1, :, 2 * width :] = ch, ch, cl
    own = pl.ds(pl.multiple_of(z * slab, slab), slab)
    total = gram[own, :]
    for d in range(1, nz):
        rcopies[d - 1].wait_recv()
        total = total + rsbuf[d]
    upd[own, :] = total
    gcopies = [send(upd.at[own], upd.at[own], ag_s.at[d], ag_r.at[d], zpeer[d]) for d in range(1, nz)]

    def fill(cat, index, value):
        high, low = split(value)
        base = index * 3 * width
        cat[:, base : base + width] = high
        cat[:, base + width : base + 2 * width] = high
        cat[:, base + 2 * width : base + 3 * width] = low

    def conjugate(cat, buffer, count):
        for m in range(count):
            high, low = split(unpack(buffer.at[m]))
            base = m * 3 * width
            value = dot(cat[:, base : base + 3 * width], jnp.concatenate([high, low, high], axis=0))
            high, low = split(value)
            ycat[:, base : base + width] = high
            ycat[:, base + width : base + 2 * width] = low
            ycat[:, base + 2 * width : base + 3 * width] = high
        span = count * 3 * width
        return dot_t(ycat[:, 0:span], cat[:, 0:span])

    for copy in gcopies:
        copy.wait_recv()
    ucopy = send(upd, upd_other, c_s.at[1], c_r.at[1], sibling)
    for copy in acopies:
        copy.wait_recv()
    group = [unpack(abuf.at[m]) for m in range(ny)]
    running = group[ny - 1]
    for m in range(ny - 2, -1, -1):
        fill(tcat, m, running)
        running = product(running, group[m])
    pack(running, bbuf.at[x])
    bcopies = [
        send(bbuf.at[x], bbuf.at[x], x_s.at[0, d], x_r.at[0, d], xpeer[d]) for d in range(1, nx)
    ]
    ucopy.wait_recv()
    mine, other = upd[...], upd_other[...]
    upd_odd = jnp.where(c == 1, mine, other)
    upd_even = jnp.where(c == 1, other, mine)
    pack(upd_odd + dot_t_full(product(odd, upd_even), odd), vbuf.at[y])
    vcopies = [
        send(vbuf.at[y], vbuf.at[y], y_s.at[1, d], y_r.at[1, d], ypeer[d]) for d in range(1, ny)
    ]
    running = jnp.where(c == 1, even, identity)
    for m in range(ny - 2, -1, -1):
        fill(kcat, m, jnp.where(m < y, running, 0.0))
        running = product(running, jnp.where(m < y, group[m], identity))
    to_band = running

    for copy in vcopies:
        copy.wait_recv()
    pack(unpack(vbuf.at[ny - 1]) + conjugate(tcat, vbuf, ny - 1), tbuf.at[x])
    tcopies = [
        send(tbuf.at[x], tbuf.at[x], x_s.at[1, d], x_r.at[1, d], xpeer[d]) for d in range(1, nx)
    ]
    front_ref[...] = jnp.where(c == 1, upd_even, 0.0) + conjugate(kcat, vbuf, ny - 1)
    for copy in bcopies:
        copy.wait_recv()
    running = to_band
    for m in range(nx - 2, -1, -1):
        fill(wcat, m, jnp.where(m < x, running, 0.0))
        if m:
            running = product(running, jnp.where(m < x, unpack(bbuf.at[m]), identity))
    for copy in tcopies:
        copy.wait_recv()
    front = front_ref[...] + conjugate(wcat, tbuf, nx - 1)
    front_ref[...] = front

    fh, fl = split(front)
    fcat[0:width, :], fcat[width : 2 * width, :], fcat[2 * width :, :] = fh, fl, fh
    sent = dot(ccat[0], fcat[...]).astype(BF16)
    p0, p1 = c * nx + x, c * ny + y
    own0 = pl.ds(pl.multiple_of(p0 * ns, ns), ns)
    own1 = pl.ds(pl.multiple_of(p1 * ns, ns), ns)
    for r in range(nr):
        x0[own0, r * half : (r + 1) * half] = sent[r * ns : (r + 1) * ns, 0:half]
    f0 = {d: send(x0.at[own0], x0.at[own0], s1_s.at[0, d], s1_r.at[0, d], xpeer[d]) for d in range(1, nx)}
    for r in range(nr):
        x1[own1, r * half : (r + 1) * half] = sent[r * ns : (r + 1) * ns, half:]
    f1 = {d: send(x1.at[own1], x1.at[own1], s1_s.at[1, d], s1_r.at[1, d], ypeer[d]) for d in range(1, ny)}
    forwards = [
        send(x0.at[own0], x0.at[own0], fw_s.at[0, 0], fw_r.at[0, 0], sibling),
        send(x1.at[own1], x1.at[own1], fw_s.at[1, 0], fw_r.at[1, 0], sibling),
    ]
    adjoint = dot(ccat[1], fcat[...])
    for h in range(2):
        gacc[h] = adjoint[:, h * half : (h + 1) * half]
    for copy in kcopies:
        copy.wait_recv()

    def selection(keys, count, bands):
        rows, lanes = count * ns, 2 * count * ns
        lane = lax.broadcasted_iota(jnp.int32, (keys.shape[1], lanes), 1) // ns
        merged = jnp.zeros((keys.shape[1], lanes), jnp.int32)
        for p in range(2 * count):
            merged = jnp.where(lane == p, keys[p], merged)
        row = lax.broadcasted_iota(jnp.int32, (rows, lanes), 0)
        wanted = row % ns
        for m in range(count):
            wanted = wanted + jnp.where(row // ns == m, bands[m] * ns, 0)
        hits = jnp.zeros((rows, lanes), F32)
        for k in range(4):
            hits = hits + jnp.where(merged[k : k + 1, :] == wanted, 1.0, 0.0)
        return hits.astype(BF16)

    sel0 = selection(keys0, ny, [at(x, m, c)["band"] for m in range(ny)])
    sel1 = selection(keys1, nx, [at(m, y, c)["band"] for m in range(nx)])

    for d in (1, 3, 2):
        if d < nx:
            f0[d].wait_recv()
            rows = pl.ds(pl.multiple_of((c * nx + (x + nx - d) % nx) * ns, ns), ns)
            forwards.append(send(x0.at[rows], x0.at[rows], fw_s.at[0, d], fw_r.at[0, d], sibling))
        if d < ny:
            f1[d].wait_recv()
            rows = pl.ds(pl.multiple_of((c * ny + (y + ny - d) % ny) * ns, ns), ns)
            forwards.append(send(x1.at[rows], x1.at[rows], fw_s.at[1, d], fw_r.at[1, d], sibling))
    for copy in forwards:
        copy.wait_recv()
    lanes = nr * half
    for q in range(lanes // width):
        span = slice(q * width, (q + 1) * width)
        o0[:, span] = dot(sel0, x0[:, span]).astype(BF16)
    last = []
    for d in range(1, ny):
        rows = pl.ds(pl.multiple_of(((y + d) % ny) * ns, ns), ns)
        last.append(send(o0.at[rows], rb0.at[d], s2_s.at[0, d], s2_r.at[0, d], ypeer[d]))
    for q in range(lanes // width):
        span = slice(q * width, (q + 1) * width)
        o1[:, span] = dot(sel1, x1[:, span]).astype(BF16)
    for d in range(1, nx):
        rows = pl.ds(pl.multiple_of(((x + d) % nx) * ns, ns), ns)
        last.append(send(o1.at[rows], rb1.at[d], s2_s.at[1, d], s2_r.at[1, d], xpeer[d]))
    for copy in last:
        copy.wait_recv()
    home0 = o0[pl.ds(pl.multiple_of(y * ns, ns), ns), :].astype(F32)
    for d in range(1, ny):
        home0 = home0 + rb0[d].astype(F32)
    home1 = o1[pl.ds(pl.multiple_of(x * ns, ns), ns), :].astype(F32)
    for d in range(1, nx):
        home1 = home1 + rb1[d].astype(F32)
    for h, home in ((0, home0), (1, home1)):
        for r in range(nr):
            place = (h, pl.ds(r, ns, stride=nr), slice(None))
            gacc[place] = gacc[place] + home[:, r * half : (r + 1) * half]
        grads_ref[:, h * half : (h + 1) * half] = gacc[h]
    for copy in started:
        copy.wait_send()


def dot_t_full(a, b):
    ah, al = split(a)
    bh, bl = split(b)
    return dot_t(ah, bh) + (dot_t(ah, bl) + dot_t(al, bh))


def body(nx, ny, panels, chain_map, couplers, anc_band, anc_slot):
    ns, width = panels.shape[2], panels.shape[3]
    nr = couplers.shape[3]
    nz = lax.axis_size("sub")
    listed = anc_band.shape[1]
    half = width // 2
    keys = (anc_band * ns + anc_slot).T
    keys = jnp.pad(keys, ((0, 8 - listed), (0, 0)), constant_values=-1)
    sources = 2 * max(nx, ny)
    keys = jnp.tile(keys, (1, sources))
    msg = (width + PAD, width)
    dma = pltpu.SemaphoreType.DMA
    scratch = [
        pltpu.VMEM((ns * width, width), BF16),
        pltpu.VMEM((width, width), F32),
        pltpu.VMEM((nz, width // nz, width), F32),
        pltpu.VMEM((width, width), F32),
        pltpu.VMEM((width, width), F32),
        pltpu.VMEM((width, width), F32),
        pltpu.VMEM((ny, *msg), BF16),
        pltpu.VMEM((nx, *msg), BF16),
        pltpu.VMEM((ny, *msg), BF16),
        pltpu.VMEM((nx, *msg), BF16),
        pltpu.VMEM((width, 3 * width * (ny - 1)), BF16),
        pltpu.VMEM((width, 3 * width * (ny - 1)), BF16),
        pltpu.VMEM((width, 3 * width * (nx - 1)), BF16),
        pltpu.VMEM((width, 3 * width * (max(nx, ny) - 1)), BF16),
        pltpu.VMEM((2, nr * ns, half), F32),
        pltpu.VMEM((nr * ns, width), F32),
        pltpu.VMEM((2, nr * ns, half), F32),
        pltpu.VMEM((2, nr * ns, 3 * width), BF16),
        pltpu.VMEM((3 * width, width), BF16),
        pltpu.VMEM((2 * nx, 8, keys.shape[1]), jnp.int32),
        pltpu.VMEM((2 * ny, 8, keys.shape[1]), jnp.int32),
        pltpu.VMEM((2 * nx * ns, nr * half), BF16),
        pltpu.VMEM((2 * ny * ns, nr * half), BF16),
        pltpu.VMEM((ny * ns, nr * half), BF16),
        pltpu.VMEM((nx * ns, nr * half), BF16),
        pltpu.VMEM((ny, ns, nr * half), BF16),
        pltpu.VMEM((nx, ns, nr * half), BF16),
        dma((8,)),
        dma((nz,)), dma((nz,)), dma((nz,)), dma((nz,)),
        dma((2,)), dma((2,)),
        dma((2, ny)), dma((2, ny)), dma((2, nx)), dma((2, nx)),
        dma((2, 4)), dma((2, 4)),
        dma((2, 4)), dma((2, 4)), dma((2, 4)), dma((2, 4)), dma((2, 4)), dma((2, 4)),
    ]
    vmem = pl.BlockSpec(memory_space=pltpu.VMEM)
    front, grads = pl.pallas_call(
        functools.partial(kernel, nx, ny, nz, ns, nr),
        out_shape=(
            jax.ShapeDtypeStruct((width, width), F32),
            jax.ShapeDtypeStruct((ns * nr, width), F32),
        ),
        in_specs=[pl.BlockSpec(memory_space=pl.ANY), vmem, vmem, vmem],
        out_specs=(vmem, vmem),
        scratch_shapes=scratch,
        compiler_params=pltpu.CompilerParams(
            collective_id=0, has_side_effects=True, vmem_limit_bytes=48 * 2**20
        ),
        name="chain",
    )(
        panels.reshape(ns * width, width),
        chain_map[0],
        couplers.reshape(ns * nr, width),
        keys,
    )
    return front[None], grads.reshape(1, 1, ns, nr, width)


def solution(mesh, nx=CHIPS_X, ny=CHIPS_Y):
    in_specs = (
        P("band", "sub", None, None, None),
        P("band", None, None),
        P("band", "sub", None, None, None),
        P(("band", "sub"), None),
        P(("band", "sub"), None),
    )
    out_specs = (P("band", None, None), P("band", "sub", None, None, None))
    return jax.shard_map(
        functools.partial(body, nx, ny), mesh=mesh, in_specs=in_specs, out_specs=out_specs, check_vma=False
    )
```

time: 505 us -> 79.9 us (0.16)
  starting transfers between devices: 220 us -> 0 us
  waiting for transfers between devices: 188 us -> 0 us
  Pallas kernels: 0 us -> 72.7 us
  matrix products: 65.4 us -> 0 us
  between operations: 14.2 us -> 0.64 us
  local copies, waits for them, and re-layouts: 11.1 us -> 5.68 us
    ppermute x31 -> x0, starting transfers between devices: 174 us -> none  [shifted(): return lax.ppermute(block, axis, route)]
    ppermute x31 -> x0, waiting for transfers between devices: 102 us -> none  [shifted(): return lax.ppermute(block, axis, route)]
    pallas_call x0 -> x1, Pallas kernels: none -> 72.7 us  [body(): pl.pallas_call(functools.partial(kernel, nx, ny, nz, ns, nr), out_shape=(...]
    dot_general x67 -> x0, matrix products: 65.4 us -> none  [the longest x31 42.1 us: apply_map(): jnp.dot(jnp.dot(matrix, state, precision=hi), matrix.T, precision=hi)]
    psum x1 -> x0, waiting for transfers between devices: 58.7 us -> none  [body(): update = lax.psum(gram / (lax.axis_size('sub') * count), 'sub')]
    all_to_all x2 -> x0, starting transfers between devices: 46.1 us -> none  [the longest x1 37.5 us: body(): lax.all_to_all(outgoing, 'band', split_axis=0, concat_axis=0, tiled=True)]
    all_to_all x2 -> x0, waiting for transfers between devices: 27 us -> none  [the longest x1 27 us: body(): lax.all_to_all(outgoing, 'band', split_axis=0, concat_axis=0, tiled=True)]
  transfers between devices with their start and end apart: 34 -> 0, of which waited for: 33 -> 0; matrix products, arithmetic and copies ran while one was open for 13% -> 0% of each run, Pallas kernels for 0% -> 0%
where the time goes in v1:
time: 79.9 us; the launch traced here: 79.7 us
  Pallas kernels  72.7 us (91%)
  local copies, waits for them, and re-layouts  5.68 us (7%)
    pallas_call x1, Pallas kernels, body(): pl.pallas_call(functools.partial(kernel, nx, ny, nz, ns, nr), out_shape=(...  72.7 us
    unnamed x8, local copies, waits for them, and re-layouts  5.58 us

profile of v1, /device:TPU:1, one launch (start us, length us, event | category | flops | bytes accessed | tf_op | source)
XLA Modules:
  0.0 79.7 jit_solution(3329718116516961262)
XLA Ops:
  0.6 0.7 add_bitcast_fusion
  1.3 0.1 tile.10.key_ref
  1.4 0.0 copy-start
  1.4 2.2 %copy-done = bf16[1,1,32,256,256]{4,3,2,1,0:T(8,128)(2,1)S(1)} copy-done((bf16[1,1,32,256,256]{4,3,2,1,0:T(8,128)(2,1)S(1)}, bf16[1,1,32,256,256]{4,3,2,1,0:T(8,128)(2,1)}, u32[]{:S(2)}) %copy-start) | copy-done | bytes 4194328
  3.6 0.0 copy-start.1
  3.6 0.9 %copy-done.1 = f32[1,256,256]{2,1,0:T(8,128)S(1)} copy-done((f32[1,256,256]{2,1,0:T(8,128)S(1)}, f32[1,256,256]{2,1,0:T(8,128)}, u32[]{:S(2)}) %copy-start.1) | copy-done | bytes 262168
  4.6 0.0 copy-start.2
  4.6 0.9 %copy-done.2 = bf16[1,1,32,16,256]{4,3,2,1,0:T(8,128)(2,1)S(1)} copy-done((bf16[1,1,32,16,256]{4,3,2,1,0:T(8,128)(2,1)S(1)}, bf16[1,1,32,16,256]{4,3,2,1,0:T(8,128)(2,1)}, u32[]{:S(2)}) %copy-start.2) | copy-done | bytes 262168
  5.5 72.7 %chain.1 = (f32[256,256]{1,0:T(8,128)S(1)}, f32[512,256]{1,0:T(8,128)S(1)}) custom-call(bf16[8192,256]{1,0:T(8,128)(2,1)S(1)} %bitcast.7, f32[256,256]{1,0:T(8,128)S(1)} %bitcast.9, bf16[512,256]{1,0:T(8,128)(2,1)S(1)} %bitcast.10, s32[8,256]{1,0:T(8,128)S(1)} %tile.10.key_ref), custom_call_target="tpu_custom_call" | custom-call | tf_op jit(solution)/shard_map/chain/pallas_call | solution.py:363
  78.2 0.7 copy.9
  78.9 0.8 copy.10
  (2 shorter events, 0.0 us)
Async XLA Ops:
  1.4 2.2 %copy-start = (bf16[1,1,32,256,256]{4,3,2,1,0:T(8,128)(2,1)S(1)}, bf16[1,1,32,256,256]{4,3,2,1,0:T(8,128)(2,1)}, u32[]{:S(2)}) copy-start(bf16[1,1,32,256,256]{4,3,2,1,0:T(8,128)(2,1)} %param.5) | copy-start | bytes 12582916
  3.6 0.9 %copy-start.1 = (f32[1,256,256]{2,1,0:T(8,128)S(1)}, f32[1,256,256]{2,1,0:T(8,128)}, u32[]{:S(2)}) copy-start(f32[1,256,256]{2,1,0:T(8,128)} %param.6) | copy-start | bytes 786436
  4.6 0.9 %copy-start.2 = (bf16[1,1,32,16,256]{4,3,2,1,0:T(8,128)(2,1)S(1)}, bf16[1,1,32,16,256]{4,3,2,1,0:T(8,128)(2,1)}, u32[]{:S(2)}) copy-start(bf16[1,1,32,16,256]{4,3,2,1,0:T(8,128)(2,1)} %param.7) | copy-start | bytes 786436

commit v2 on v1

v2 whole, which is shorter than its diff:
```python
import functools

import jax
import jax.numpy as jnp
from jax import lax
from jax.experimental import pallas as pl
from jax.experimental.pallas import tpu as pltpu
from jax.sharding import PartitionSpec as P

MESH = pl.DeviceIdType.MESH
F32, BF16 = jnp.float32, jnp.bfloat16
CHIPS_X, CHIPS_Y = 4, 4
PAD = 16
CHUNKS = 2


def split(value):
    high = value.astype(BF16)
    return high, (value - high.astype(F32)).astype(BF16)


def dot(a, b):
    return jnp.dot(a, b, preferred_element_type=F32)


def dot_t(a, b):
    return lax.dot_general(a, b, (((1,), (1,)), ((), ())), preferred_element_type=F32)


def product(a, b):
    ah, al = split(a)
    bh, bl = split(b)
    return dot(ah, bh) + (dot(ah, bl) + dot(al, bh))


def product_t(a, b):
    ah, al = split(a)
    bh, bl = split(b)
    return dot_t(ah, bh) + (dot_t(ah, bl) + dot_t(al, bh))


def grid(shape, axis):
    return lax.broadcasted_iota(jnp.int32, shape, axis)


def diagonal(width):
    return grid((width, width), 0) == grid((width, width), 1)


def pick(block):
    return jnp.sum(jnp.where(diagonal(block.shape[0]), block, 0.0), axis=0, keepdims=True)


def pack_map(value, message):
    width = value.shape[1]
    high = value.astype(BF16)
    rest = pick(value - high.astype(F32))
    message[0:width, :] = high
    message[width : width + PAD, :] = jnp.broadcast_to(rest, (PAD, width)).astype(BF16)


def unpack_map(message):
    width = message.shape[1]
    rest = message[width : width + PAD, :].astype(F32)[0:1, :]
    return message[0:width, :].astype(F32) + jnp.where(diagonal(width), rest, 0.0)


def halves(full):
    half = full.shape[0] // 2
    upper = grid((half, half), 0) <= grid((half, half), 1)
    low = full[half:, half:]
    return full[:half, half:], jnp.where(upper, full[:half, :half], low), pick(low)


def halves_of_sum(full):
    half = full.shape[0] // 2
    rows, cols = grid((half, half), 0), grid((half, half), 1)
    first, low = full[:half, :half], full[half:, half:]
    side = full[:half, half:] + full[half:, :half].T
    mixed = jnp.where(rows <= cols, first, low) + jnp.where(rows >= cols, first, low).T
    return side, mixed, 2.0 * pick(low)


def one_sided(side, mixed, last):
    half = side.shape[0]
    rows, cols = grid((half, half), 0), grid((half, half), 1)
    middle = rows == cols
    first = jnp.where(rows < cols, mixed, jnp.where(middle, 0.5 * mixed, 0.0))
    low = jnp.where(rows > cols, mixed, jnp.where(middle, 0.5 * last, 0.0))
    top = jnp.concatenate([first, side], axis=1)
    return jnp.concatenate([top, jnp.concatenate([jnp.zeros_like(side), low], axis=1)], axis=0)


def pack(parts, message):
    side, mixed, last = parts
    half = side.shape[0]
    message[0:half, 0:half] = side.astype(BF16)
    high = mixed.astype(BF16)
    message[0:half, half:] = high
    rest = pick(mixed - high.astype(F32))
    last_high = last.astype(BF16).astype(F32)
    row = grid((PAD, half), 0)
    message[half : half + PAD, 0:half] = jnp.where(row == 0, rest, 0.0).astype(BF16)
    tail = jnp.where(row == 0, last - last_high, jnp.where(row == 1, last_high, 0.0))
    message[half : half + PAD, half:] = tail.astype(BF16)


def unpack(message):
    half = message.shape[1] // 2
    tail = message[half : half + PAD, :].astype(F32)
    rest = tail[0:1, 0:half]
    mixed = message[0:half, half:].astype(F32) + jnp.where(diagonal(half), rest, 0.0)
    return message[0:half, 0:half].astype(F32), mixed, tail[0:1, half:] + tail[1:2, half:]


def kernel(
    nx, ny, nz, ns, nr,
    panels, map_hbm, coup_hbm, key_hbm,
    front_ref, grads_ref,
    pv, map_ref, coup_ref, key_ref, gram, ends, rsbuf, upd, upd_other, map_other, abuf, bbuf, vbuf, tbuf,
    tcat, kcat, wcat, ycat, own_front, crm, cjm, gacc, ccat, fcat,
    keys0, keys1, xs0, xs1, x0, x1, sel0, sel1, o0, o1, rb0, rb1,
    psem, isem, rs_s, rs_r, dg_s, dg_r, ag_s, ag_r, c_s, c_r, y_s, y_r, x_s, x_r, k_s, k_r,
    s1_s, s1_r, s2_s, s2_r,
):
    width = map_ref.shape[0]
    half = width // 2
    slab = half // nz
    band, z = lax.axis_index("band"), lax.axis_index("sub")
    x, y, c = band // (2 * ny), (band // 2) % ny, band % 2

    def at(xx, yy, cc):
        return {"band": (xx * ny + yy) * 2 + cc}

    cores = (c, 1 - c)
    sibling = at(x, y, 1 - c)
    xpeer = {(d, e): at((x + d) % nx, y, cores[e]) for d in range(1, nx) for e in range(2)}
    ypeer = {(d, e): at(x, (y + d) % ny, cores[e]) for d in range(1, ny) for e in range(2)}
    zpeer = {d: {"sub": (z + d) % nz} for d in range(1, nz)}
    peers = [sibling, *xpeer.values(), *ypeer.values(), *zpeer.values()]
    started = []

    def send(src, dst, s, r, target):
        copy = pltpu.make_async_remote_copy(
            src_ref=src, dst_ref=dst, send_sem=s, recv_sem=r, device_id=target, device_id_type=MESH
        )
        copy.start()
        started.append(copy)
        return copy

    barrier = pltpu.get_barrier_semaphore()
    for peer in peers:
        pl.semaphore_signal(barrier, inc=1, device_id=peer, device_id_type=MESH)
    chunks = psem.shape[0]
    per = ns // chunks
    loads = []
    for q in range(chunks):
        rows = pl.ds(q * per * width, per * width)
        loads.append(pltpu.make_async_copy(panels.at[rows], pv.at[rows], psem.at[q]))
        loads[-1].start()
        if q == 0:
            inputs = []
            for n, (src, dst) in enumerate(((coup_hbm, coup_ref), (map_hbm, map_ref), (key_hbm, key_ref))):
                inputs.append(pltpu.make_async_copy(src, dst, isem.at[n]))
                inputs[-1].start()
    inputs[0].wait()
    for q in range(chunks):
        loads[q].wait()
        block = pv[q * per * width : (q + 1) * per * width, :]
        part = dot(block.T, block)
        gram[...] = part if q == 0 else gram[...] + part
        for j in range(q * per, (q + 1) * per):
            value = dot(coup_ref[j * nr : (j + 1) * nr, :], pv[j * width : (j + 1) * width, :])
            cjm[j * nr : (j + 1) * nr, :] = value
            for h in range(2):
                crm[h, pl.ds(j, nr, stride=ns), :] = value[:, h * half : (h + 1) * half]
    side, mixed, last = halves(gram[...] * (1.0 / (nz * ns)))
    gram[0:half, 0:half] = side
    gram[0:half, half:] = mixed
    ends[pl.ds(z, 1)] = jnp.broadcast_to(last, (8, half))[None]
    inputs[1].wait()
    inputs[2].wait()
    pl.semaphore_wait(barrier, len(peers))

    rcopies = [
        send(gram.at[pl.ds(((z + d) % nz) * slab, slab)], rsbuf.at[d], rs_s.at[d], rs_r.at[d], zpeer[d])
        for d in range(1, nz)
    ]
    maps = send(map_ref, map_other, c_s.at[0], c_r.at[0], sibling)
    dcopies = [send(ends.at[z], ends.at[z], dg_s.at[d], dg_r.at[d], zpeer[d]) for d in range(1, nz)]
    p0, p1 = c * nx + x, c * ny + y
    keys0[pl.ds(p0, 1)] = key_ref[...][None]
    keys1[pl.ds(p1, 1)] = key_ref[...][None]
    own = keys0.at[p0]
    kcopies = [send(own, own, k_s.at[0, 0, 1], k_r.at[0, 0, 1], sibling)]
    for (d, e), peer in xpeer.items():
        kcopies.append(send(own, own, k_s.at[0, d, e], k_r.at[0, d, e], peer))
    own = keys1.at[p1]
    kcopies.append(send(own, own, k_s.at[1, 0, 1], k_r.at[1, 0, 1], sibling))
    for (d, e), peer in ypeer.items():
        kcopies.append(send(own, own, k_s.at[1, d, e], k_r.at[1, d, e], peer))
    maps.wait_recv()
    mine, other = map_ref[...], map_other[...]
    odd = jnp.where(c == 1, mine, other)
    even = jnp.where(c == 1, other, mine)
    identity = diagonal(width).astype(F32)
    pack_map(product(odd, even), abuf.at[y])
    acopies = [
        send(abuf.at[y], abuf.at[y], y_s.at[0, d], y_r.at[0, d], ypeer[d, 0]) for d in range(1, ny)
    ]
    ch, cl = split(jnp.concatenate([crm[0], crm[1]], axis=1))
    ccat[0, :, 0:width], ccat[0, :, width : 2 * width], ccat[0, :, 2 * width :] = ch, ch, cl
    ch, cl = split(cjm[...])
    ccat[1, :, 0:width], ccat[1, :, width : 2 * width], ccat[1, :, 2 * width :] = ch, ch, cl
    own = pl.ds(pl.multiple_of(z * slab, slab), slab)
    total = gram[own, :]
    for d in range(1, nz):
        rcopies[d - 1].wait_recv()
        total = total + rsbuf[d]
    upd[own, :] = total
    gcopies = [send(upd.at[own], upd.at[own], ag_s.at[d], ag_r.at[d], zpeer[d]) for d in range(1, nz)]
    for copy in dcopies:
        copy.wait_recv()
    last = ends[0]
    for m in range(1, nz):
        last = last + ends[m]
    upd[half : half + 8, 0:half] = last
    upd[half : half + 8, half:] = jnp.zeros_like(last)

    def fill(cat, index, value):
        high, low = split(value)
        base = index * 3 * width
        cat[:, base : base + width] = high
        cat[:, base + width : base + 2 * width] = high
        cat[:, base + 2 * width : base + 3 * width] = low

    def conjugate(cat, buffer, count):
        for m in range(count):
            high, low = split(one_sided(*unpack(buffer.at[m])))
            base = m * 3 * width
            value = dot(cat[:, base : base + 3 * width], jnp.concatenate([high, low, high], axis=0))
            high, low = split(value)
            ycat[:, base : base + width] = high
            ycat[:, base + width : base + 2 * width] = low
            ycat[:, base + 2 * width : base + 3 * width] = high
        span = count * 3 * width
        return dot_t(ycat[:, 0:span], cat[:, 0:span])

    for copy in acopies:
        copy.wait_recv()
    group = [unpack_map(abuf.at[m]) for m in range(ny)]
    running = group[ny - 1]
    for m in range(ny - 2, -1, -1):
        fill(tcat, m, running)
        running = product(running, group[m])
    pack_map(running, bbuf.at[x])
    bcopies = [
        send(bbuf.at[x], bbuf.at[x], x_s.at[0, d], x_r.at[0, d], xpeer[d, 0]) for d in range(1, nx)
    ]
    for copy in gcopies:
        copy.wait_recv()
    ucopy = send(upd, upd_other, c_s.at[1], c_r.at[1], sibling)
    ucopy.wait_recv()
    mine, other = upd[...], upd_other[...]
    upd_odd = jnp.where(c == 1, mine, other)
    upd_even = jnp.where(c == 1, other, mine)
    upd_even = one_sided(upd_even[0:half, 0:half], upd_even[0:half, half:], upd_even[half : half + 1, 0:half])
    side, mixed, last = halves_of_sum(product_t(product(odd, upd_even), odd))
    side, mixed = side + upd_odd[0:half, 0:half], mixed + upd_odd[0:half, half:]
    pack((side, mixed, last + upd_odd[half : half + 1, 0:half]), vbuf.at[y])
    vcopies = [
        send(vbuf.at[y], vbuf.at[y], y_s.at[1, d], y_r.at[1, d], ypeer[d, 0]) for d in range(1, ny)
    ]
    running = jnp.where(c == 1, even, identity)
    for m in range(ny - 2, -1, -1):
        fill(kcat, m, jnp.where(m < y, running, 0.0))
        running = product(running, jnp.where(m < y, group[m], identity))
    to_band = running

    for copy in vcopies:
        copy.wait_recv()
    side, mixed, last = unpack(vbuf.at[ny - 1])
    more_side, more_mixed, more_last = halves_of_sum(conjugate(tcat, vbuf, ny - 1))
    pack((side + more_side, mixed + more_mixed, last + more_last), tbuf.at[x])
    tcopies = [
        send(tbuf.at[x], tbuf.at[x], x_s.at[1, d], x_r.at[1, d], xpeer[d, 0]) for d in range(1, nx)
    ]
    own_front[...] = jnp.where(c == 1, upd_even, 0.0) + conjugate(kcat, vbuf, ny - 1)
    for copy in bcopies:
        copy.wait_recv()
    running = to_band
    for m in range(nx - 2, -1, -1):
        fill(wcat, m, jnp.where(m < x, running, 0.0))
        if m:
            running = product(running, jnp.where(m < x, unpack_map(bbuf.at[m]), identity))
    for copy in kcopies:
        copy.wait_recv()

    def selection(keys, count, band_of):
        rows, lanes = 2 * count * ns, 2 * count * ns
        lane = grid((8, lanes), 1) // ns
        merged = jnp.zeros((8, lanes), jnp.int32)
        for p in range(2 * count):
            merged = jnp.where(lane == p, keys[p, :, 0:lanes], merged)
        row = grid((rows, lanes), 0)
        wanted = row % ns
        for p in range(2 * count):
            target = band_of(p % count, p // count)["band"]
            wanted = wanted + jnp.where(row // ns == p, target * ns, 0)
        hits = jnp.zeros((rows, lanes), F32)
        for k in range(4):
            hits = hits + jnp.where(merged[k : k + 1, :] == wanted, 1.0, 0.0)
        return hits.astype(BF16)

    sel0[...] = selection(keys0, ny, lambda m, core: at(x, m, core))
    sel1[...] = selection(keys1, nx, lambda m, core: at(m, y, core))
    for copy in tcopies:
        copy.wait_recv()
    front = own_front[...] + conjugate(wcat, tbuf, nx - 1)
    front = front + front.T
    front_ref[...] = front

    fh, fl = split(front)
    fcat[0:width, :], fcat[width : 2 * width, :], fcat[2 * width :, :] = fh, fl, fh
    lanes = nr * half // 2
    piece = lanes // CHUNKS
    own0 = pl.ds(pl.multiple_of(p0 * ns, ns), ns)
    own1 = pl.ds(pl.multiple_of(p1 * ns, ns), ns)
    gathers = []
    for q in range(CHUNKS):
        span = pl.ds(q * piece, piece)
        for core in range(2):
            first = (core * CHUNKS + q) * (nr // 2 // CHUNKS)
            count = nr // 2 // CHUNKS
            sent = dot(ccat[0, first * ns : (first + count) * ns, :], fcat[...]).astype(BF16)
            for r in range(count):
                place = slice(q * piece + r * half, q * piece + (r + 1) * half)
                xs0[core, :, place] = sent[r * ns : (r + 1) * ns, 0:half]
                xs1[core, :, place] = sent[r * ns : (r + 1) * ns, half:]
        batch = {}
        for h, xs, xx, rows, all_peers in ((0, xs0, x0, own0, xpeer), (1, xs1, x1, own1, ypeer)):
            batch[h] = []
            targets = {**all_peers, (0, 1): sibling}
            for (d, e), peer in targets.items():
                batch[h].append(
                    send(
                        xs.at[cores[e], :, span], xx.at[rows, span],
                        s1_s.at[q, h, d, e], s1_r.at[q, h, d, e], peer,
                    )
                )
            xx[rows, span] = xs[c, :, span]
        gathers.append(batch)
    adjoint = dot(ccat[1], fcat[...])
    for h in range(2):
        gacc[h] = adjoint[:, h * half : (h + 1) * half]
    scatters = []
    for q in range(CHUNKS):
        for h, sel, xx, oo, rb, count, all_peers in (
            (0, sel0, x0, o0, rb0, ny, ypeer), (1, sel1, x1, o1, rb1, nx, xpeer),
        ):
            here = (y, x)[h]
            for copy in gathers[q][h]:
                copy.wait_recv()
            for first in range(q * piece, (q + 1) * piece, width):
                span = slice(first, first + width)
                oo[:, span] = dot(sel[...], xx[:, span]).astype(BF16)
            span = pl.ds(q * piece, piece)
            for (d, e), peer in {**all_peers, (0, 1): sibling}.items():
                rows = pl.ds(pl.multiple_of((cores[e] * count + (here + d) % count) * ns, ns), ns)
                scatters.append(
                    send(
                        oo.at[rows, span], rb.at[d, e, :, span],
                        s2_s.at[q, h, d, e], s2_r.at[q, h, d, e], peer,
                    )
                )
    for copy in scatters:
        copy.wait_recv()
    for h, oo, rb, count, here in ((0, o0, rb0, ny, y), (1, o1, rb1, nx, x)):
        rows = pl.ds(pl.multiple_of((c * count + here) * ns, ns), ns)
        same, cross = oo[rows, :].astype(F32), rb[0, 1].astype(F32)
        for d in range(1, count):
            same, cross = same + rb[d, 0].astype(F32), cross + rb[d, 1].astype(F32)
        parts = jnp.where(c == 0, same, cross), jnp.where(c == 0, cross, same)
        for r in range(nr):
            place = (h, pl.ds(r, ns, stride=nr), slice(None))
            lane = r % (nr // 2) * half
            gacc[place] = gacc[place] + parts[r // (nr // 2)][:, lane : lane + half]
        grads_ref[:, h * half : (h + 1) * half] = gacc[h]
    for copy in started:
        copy.wait_send()


def body(nx, ny, panels, chain_map, couplers, anc_band, anc_slot):
    ns, width = panels.shape[2], panels.shape[3]
    nr = couplers.shape[3]
    nz = lax.axis_size("sub")
    listed = anc_band.shape[1]
    half = width // 2
    keys = (anc_band * ns + anc_slot).T
    keys = jnp.pad(keys, ((0, 8 - listed), (0, 0)), constant_values=-1)
    keys = jnp.tile(keys, (1, 2 * max(nx, ny)))
    lanes = nr * half // 2
    mapmsg, symmsg = (width + PAD, width), (half + PAD, width)
    far = max(nx, ny)
    dma = lambda *shape: pltpu.SemaphoreType.DMA(shape)
    scratch = [
        pltpu.VMEM((ns * width, width), BF16),
        pltpu.VMEM((width, width), F32),
        pltpu.VMEM((nr * ns, width), BF16),
        pltpu.VMEM(keys.shape, jnp.int32),
        pltpu.VMEM((width, width), F32),
        pltpu.VMEM((nz, 8, half), F32),
        pltpu.VMEM((nz, half // nz, width), F32),
        pltpu.VMEM((half + 8, width), F32),
        pltpu.VMEM((half + 8, width), F32),
        pltpu.VMEM((width, width), F32),
        pltpu.VMEM((ny, *mapmsg), BF16),
        pltpu.VMEM((nx, *mapmsg), BF16),
        pltpu.VMEM((ny, *symmsg), BF16),
        pltpu.VMEM((nx, *symmsg), BF16),
        pltpu.VMEM((width, 3 * width * (ny - 1)), BF16),
        pltpu.VMEM((width, 3 * width * (ny - 1)), BF16),
        pltpu.VMEM((width, 3 * width * (nx - 1)), BF16),
        pltpu.VMEM((width, 3 * width * (far - 1)), BF16),
        pltpu.VMEM((width, width), F32),
        pltpu.VMEM((2, nr * ns, half), F32),
        pltpu.VMEM((nr * ns, width), F32),
        pltpu.VMEM((2, nr * ns, half), F32),
        pltpu.VMEM((2, nr * ns, 3 * width), BF16),
        pltpu.VMEM((3 * width, width), BF16),
        pltpu.VMEM((2 * nx, *keys.shape), jnp.int32),
        pltpu.VMEM((2 * ny, *keys.shape), jnp.int32),
        pltpu.VMEM((2, ns, lanes), BF16),
        pltpu.VMEM((2, ns, lanes), BF16),
        pltpu.VMEM((2 * nx * ns, lanes), BF16),
        pltpu.VMEM((2 * ny * ns, lanes), BF16),
        pltpu.VMEM((2 * ny * ns, 2 * ny * ns), BF16),
        pltpu.VMEM((2 * nx * ns, 2 * nx * ns), BF16),
        pltpu.VMEM((2 * ny * ns, lanes), BF16),
        pltpu.VMEM((2 * nx * ns, lanes), BF16),
        pltpu.VMEM((ny, 2, ns, lanes), BF16),
        pltpu.VMEM((nx, 2, ns, lanes), BF16),
        dma(8), dma(3),
        dma(nz), dma(nz), dma(nz), dma(nz), dma(nz), dma(nz),
        dma(2), dma(2),
        dma(2, ny), dma(2, ny), dma(2, nx), dma(2, nx),
        dma(2, far, 2), dma(2, far, 2),
        dma(CHUNKS, 2, far, 2), dma(CHUNKS, 2, far, 2), dma(CHUNKS, 2, far, 2), dma(CHUNKS, 2, far, 2),
    ]
    vmem = pl.BlockSpec(memory_space=pltpu.VMEM)
    hbm = pl.BlockSpec(memory_space=pl.ANY)
    front, grads = pl.pallas_call(
        functools.partial(kernel, nx, ny, nz, ns, nr),
        out_shape=(
            jax.ShapeDtypeStruct((width, width), F32),
            jax.ShapeDtypeStruct((ns * nr, width), F32),
        ),
        in_specs=[hbm] * 4,
        out_specs=(vmem, vmem),
        scratch_shapes=scratch,
        compiler_params=pltpu.CompilerParams(
            collective_id=0, has_side_effects=True, vmem_limit_bytes=56 * 2**20
        ),
        name="chain",
    )(
        panels.reshape(ns * width, width),
        chain_map[0],
        couplers.reshape(ns * nr, width),
        keys,
    )
    return front[None], grads.reshape(1, 1, ns, nr, width)


def solution(mesh, nx=CHIPS_X, ny=CHIPS_Y):
    in_specs = (
        P("band", "sub", None, None, None),
        P("band", None, None),
        P("band", "sub", None, None, None),
        P(("band", "sub"), None),
        P(("band", "sub"), None),
    )
    out_specs = (P("band", None, None), P("band", "sub", None, None, None))
    return jax.shard_map(
        functools.partial(body, nx, ny), mesh=mesh, in_specs=in_specs, out_specs=out_specs, check_vma=False
    )
```

time: 79.9 us -> 63.1 us (0.79)
  Pallas kernels: 72.7 us -> 57.3 us
  local copies, waits for them, and re-layouts: 5.68 us -> 4.23 us
    pallas_call x1, Pallas kernels: 72.7 us -> 57.3 us  [body(): pl.pallas_call(functools.partial(kernel, nx, ny, nz, ns, nr), out_shape=(...]
    unnamed x8 -> x2, local copies, waits for them, and re-layouts: 5.58 us -> 3.54 us
where the time goes in v2:
time: 63.1 us; the launch traced here: 62.9 us
  Pallas kernels  57.3 us (91%)
  local copies, waits for them, and re-layouts  4.23 us (7%)
  other arithmetic  0.7 us (1%)
  between operations  0.64 us (1%)
    pallas_call x1, Pallas kernels, body(): pl.pallas_call(functools.partial(kernel, nx, ny, nz, ns, nr), out_shape=(...  57.3 us
    unnamed x2, local copies, waits for them, and re-layouts  3.54 us

profile of v2, /device:TPU:1, one launch (start us, length us, event | category | flops | bytes accessed | tf_op | source)
XLA Modules:
  0.0 62.9 jit_solution(17660786376419948037)
XLA Ops:
  0.6 0.7 %add_bitcast_fusion = s32[4,32]{1,0:T(4,128)S(1)} fusion(s32[32,4]{0,1:T(4,128)} %param.9, s32[32,4]{0,1:T(4,128)} %param.8), kind=kLoop, calls=%fused_computation | loop fusion | flops 256 | bytes 1536 | tf_op jit(solution)/shard_map/transpose | solution.py:399
  1.3 0.7 %tile.10.key_hbm = s32[8,256]{1,0:T(8,128)} reshape(s32[8,8,32]{2,1,0:T(8,128)S(1)} %tile.4) | data formatting | bytes 16384 | tf_op jit(solution)/shard_map/tile | solution.py:401
  2.0 57.3 %chain.1 = (f32[256,256]{1,0:T(8,128)}, f32[512,256]{1,0:T(8,128)}) custom-call(bf16[8192,256]{1,0:T(8,128)(2,1)} %bitcast.7, f32[256,256]{1,0:T(8,128)} %bitcast.9, bf16[512,256]{1,0:T(8,128)(2,1)} %bitcast.10, s32[8,256]{1,0:T(8,128)} %tile.10.key_hbm), custom_call_target="tpu_custom_call" | custom-call | tf_op jit(solution)/shard_map/chain/pallas_call | solution.py:452
  59.4 1.7 %copy.9 = f32[1,256,256]{2,1,0:T(8,128)} copy(f32[1,256,256]{2,1,0:T(8,128)} %bitcast.11) | data formatting | bytes 524288
  61.0 1.9 %copy.10 = f32[1,1,32,16,256]{4,3,2,1,0:T(8,128)} copy(f32[1,1,32,16,256]{4,3,2,1,0:T(8,128)} %bitcast.8) | data formatting | bytes 1048576
  (2 shorter events, 0.0 us)

commit v3 on v2

--- a/solution.py
+++ b/solution.py
@@ -115,9 +115,9 @@
 
 def kernel(
     nx, ny, nz, ns, nr,
-    panels, map_hbm, coup_hbm, key_hbm,
+    panels, map_hbm, coup_hbm, band_hbm, slot_hbm,
     front_ref, grads_ref,
-    pv, map_ref, coup_ref, key_ref, gram, ends, rsbuf, upd, upd_other, map_other, abuf, bbuf, vbuf, tbuf,
+    pv, map_ref, coup_ref, band_ref, slot_ref, gram, ends, rsbuf, upd, upd_other, map_other, abuf, bbuf, vbuf, tbuf,
     tcat, kcat, wcat, ycat, own_front, crm, cjm, gacc, ccat, fcat,
     keys0, keys1, xs0, xs1, x0, x1, sel0, sel1, o0, o1, rb0, rb1,
     psem, isem, rs_s, rs_r, dg_s, dg_r, ag_s, ag_r, c_s, c_r, y_s, y_r, x_s, x_r, k_s, k_r,
@@ -160,7 +160,8 @@
         loads[-1].start()
         if q == 0:
             inputs = []
-            for n, (src, dst) in enumerate(((coup_hbm, coup_ref), (map_hbm, map_ref), (key_hbm, key_ref))):
+            small = ((coup_hbm, coup_ref), (map_hbm, map_ref), (band_hbm, band_ref), (slot_hbm, slot_ref))
+            for n, (src, dst) in enumerate(small):
                 inputs.append(pltpu.make_async_copy(src, dst, isem.at[n]))
                 inputs[-1].start()
     inputs[0].wait()
@@ -178,8 +179,8 @@
     gram[0:half, 0:half] = side
     gram[0:half, half:] = mixed
     ends[pl.ds(z, 1)] = jnp.broadcast_to(last, (8, half))[None]
-    inputs[1].wait()
-    inputs[2].wait()
+    for copy in inputs[1:]:
+        copy.wait()
     pl.semaphore_wait(barrier, len(peers))
 
     rcopies = [
@@ -189,8 +190,11 @@
     maps = send(map_ref, map_other, c_s.at[0], c_r.at[0], sibling)
     dcopies = [send(ends.at[z], ends.at[z], dg_s.at[d], dg_r.at[d], zpeer[d]) for d in range(1, nz)]
     p0, p1 = c * nx + x, c * ny + y
-    keys0[pl.ds(p0, 1)] = key_ref[...][None]
-    keys1[pl.ds(p1, 1)] = key_ref[...][None]
+    keys = band_ref[...] * ns + slot_ref[...]
+    keys = jnp.concatenate([keys, jnp.full((8 - keys.shape[0], ns), -1, jnp.int32)], axis=0)
+    keys = jnp.concatenate([keys] * (keys0.shape[2] // ns), axis=1)
+    keys0[pl.ds(p0, 1)] = keys[None]
+    keys1[pl.ds(p1, 1)] = keys[None]
     own = keys0.at[p0]
     kcopies = [send(own, own, k_s.at[0, 0, 1], k_r.at[0, 0, 1], sibling)]
     for (d, e), peer in xpeer.items():
@@ -246,17 +250,6 @@
         span = count * 3 * width
         return dot_t(ycat[:, 0:span], cat[:, 0:span])
 
-    for copy in acopies:
-        copy.wait_recv()
-    group = [unpack_map(abuf.at[m]) for m in range(ny)]
-    running = group[ny - 1]
-    for m in range(ny - 2, -1, -1):
-        fill(tcat, m, running)
-        running = product(running, group[m])
-    pack_map(running, bbuf.at[x])
-    bcopies = [
-        send(bbuf.at[x], bbuf.at[x], x_s.at[0, d], x_r.at[0, d], xpeer[d, 0]) for d in range(1, nx)
-    ]
     for copy in gcopies:
         copy.wait_recv()
     ucopy = send(upd, upd_other, c_s.at[1], c_r.at[1], sibling)
@@ -270,6 +263,17 @@
     pack((side, mixed, last + upd_odd[half : half + 1, 0:half]), vbuf.at[y])
     vcopies = [
         send(vbuf.at[y], vbuf.at[y], y_s.at[1, d], y_r.at[1, d], ypeer[d, 0]) for d in range(1, ny)
+    ]
+    for copy in acopies:
+        copy.wait_recv()
+    group = [unpack_map(abuf.at[m]) for m in range(ny)]
+    running = group[ny - 1]
+    for m in range(ny - 2, -1, -1):
+        fill(tcat, m, running)
+        running = product(running, group[m])
+    pack_map(running, bbuf.at[x])
+    bcopies = [
+        send(bbuf.at[x], bbuf.at[x], x_s.at[0, d], x_r.at[0, d], xpeer[d, 0]) for d in range(1, nx)
     ]
     running = jnp.where(c == 1, even, identity)
     for m in range(ny - 2, -1, -1):
@@ -396,9 +400,7 @@
     nz = lax.axis_size("sub")
     listed = anc_band.shape[1]
     half = width // 2
-    keys = (anc_band * ns + anc_slot).T
-    keys = jnp.pad(keys, ((0, 8 - listed), (0, 0)), constant_values=-1)
-    keys = jnp.tile(keys, (1, 2 * max(nx, ny)))
+    sources = 2 * max(nx, ny)
     lanes = nr * half // 2
     mapmsg, symmsg = (width + PAD, width), (half + PAD, width)
     far = max(nx, ny)
@@ -407,7 +409,8 @@
         pltpu.VMEM((ns * width, width), BF16),
         pltpu.VMEM((width, width), F32),
         pltpu.VMEM((nr * ns, width), BF16),
-        pltpu.VMEM(keys.shape, jnp.int32),
+        pltpu.VMEM((listed, ns), jnp.int32),
+        pltpu.VMEM((listed, ns), jnp.int32),
         pltpu.VMEM((width, width), F32),
         pltpu.VMEM((nz, 8, half), F32),
         pltpu.VMEM((nz, half // nz, width), F32),
@@ -428,8 +431,8 @@
         pltpu.VMEM((2, nr * ns, half), F32),
         pltpu.VMEM((2, nr * ns, 3 * width), BF16),
         pltpu.VMEM((3 * width, width), BF16),
-        pltpu.VMEM((2 * nx, *keys.shape), jnp.int32),
-        pltpu.VMEM((2 * ny, *keys.shape), jnp.int32),
+        pltpu.VMEM((2 * nx, 8, sources * ns), jnp.int32),
+        pltpu.VMEM((2 * ny, 8, sources * ns), jnp.int32),
         pltpu.VMEM((2, ns, lanes), BF16),
         pltpu.VMEM((2, ns, lanes), BF16),
         pltpu.VMEM((2 * nx * ns, lanes), BF16),
@@ -440,7 +443,7 @@
         pltpu.VMEM((2 * nx * ns, lanes), BF16),
         pltpu.VMEM((ny, 2, ns, lanes), BF16),
         pltpu.VMEM((nx, 2, ns, lanes), BF16),
-        dma(8), dma(3),
+        dma(8), dma(4),
         dma(nz), dma(nz), dma(nz), dma(nz), dma(nz), dma(nz),
         dma(2), dma(2),
         dma(2, ny), dma(2, ny), dma(2, nx), dma(2, nx),
@@ -455,18 +458,24 @@
             jax.ShapeDtypeStruct((width, width), F32),
             jax.ShapeDtypeStruct((ns * nr, width), F32),
         ),
-        in_specs=[hbm] * 4,
+        in_specs=[hbm] * 5,
         out_specs=(vmem, vmem),
         scratch_shapes=scratch,
         compiler_params=pltpu.CompilerParams(
-            collective_id=0, has_side_effects=True, vmem_limit_bytes=56 * 2**20
+            collective_id=0, has_side_effects=True, vmem_limit_bytes=48 * 2**20
         ),
         name="chain",
     )(
-        panels.reshape(ns * width, width),
-        chain_map[0],
-        couplers.reshape(ns * nr, width),
-        keys,
+        *(
+            pltpu.with_memory_space_constraint(array, pltpu.HBM)
+            for array in (
+                panels.reshape(ns * width, width),
+                chain_map[0],
+                couplers.reshape(ns * nr, width),
+                anc_band.T,
+                anc_slot.T,
+            )
+        )
     )
     return front[None], grads.reshape(1, 1, ns, nr, width)
 

time: 63.1 us -> 58.9 us (0.933)
  local copies, waits for them, and re-layouts: 4.23 us -> 1.5 us
  other arithmetic: 0.7 us -> 0 us
    unnamed x2, local copies, waits for them, and re-layouts: 3.54 us -> 1.5 us
    transpose x1 -> x0, other arithmetic: 0.7 us -> none  [body(): keys = (anc_band * ns + anc_slot).T]
    another operation x2 -> x0, local copies, waits for them, and re-layouts: 0.68 us -> none  [body(): keys = jnp.tile(keys, (1, 2 * max(nx, ny)))]
where the time goes in v3:
time: 58.9 us
  Pallas kernels  56.7 us (96%)
  local copies, waits for them, and re-layouts  1.5 us (3%)
  between operations  0.64 us (1%)
    pallas_call x1, Pallas kernels, body(): pl.pallas_call(functools.partial(kernel, nx, ny, nz, ns, nr), out_shape=(...  56.7 us
    unnamed x2, local copies, waits for them, and re-layouts  1.5 us

profile of v3, /device:TPU:1, one launch (start us, length us, event | category | flops | bytes accessed | tf_op | source)
XLA Modules:
  0.0 58.9 jit_solution(1430083480298147295)
XLA Ops:
  0.6 56.7 %chain.1 = (f32[256,256]{1,0:T(8,128)S(1)}, f32[512,256]{1,0:T(8,128)S(1)}) custom-call(bf16[8192,256]{1,0:T(8,128)(2,1)} %bitcast.9, f32[256,256]{1,0:T(8,128)} %bitcast.10, bf16[512,256]{1,0:T(8,128)(2,1)} %bitcast.11, s32[4,32]{1,0:T(4,128)} %bitcast.12, s32[4,32]{1,0:T(4,128)} %bitcast.13), custom_call_target="tpu_custom_call" | custom-call | tf_op jit(solution)/shard_map/chain/pallas_call | solution.py:455
  57.4 0.7 %copy.9 = f32[1,256,256]{2,1,0:T(8,128)} copy(f32[1,256,256]{2,1,0:T(8,128)S(1)} %bitcast.8) | data formatting | bytes 524288
  58.1 0.8 %copy.10 = f32[1,1,32,16,256]{4,3,2,1,0:T(8,128)} copy(f32[1,1,32,16,256]{4,3,2,1,0:T(8,128)S(1)} %bitcast.7) | data formatting | bytes 1048576

commit v4 on v3

--- a/solution.py
+++ b/solution.py
@@ -12,6 +12,7 @@
 CHIPS_X, CHIPS_Y = 4, 4
 PAD = 16
 CHUNKS = 2
+AHEAD = 3
 
 
 def split(value):
@@ -113,12 +114,16 @@
     return message[0:half, 0:half].astype(F32), mixed, tail[0:1, half:] + tail[1:2, half:]
 
 
+def far_first(count):
+    return sorted(range(1, count), key=lambda d: -min(d, count - d))
+
+
 def kernel(
     nx, ny, nz, ns, nr,
     panels, map_hbm, coup_hbm, band_hbm, slot_hbm,
     front_ref, grads_ref,
     pv, map_ref, coup_ref, band_ref, slot_ref, gram, ends, rsbuf, upd, upd_other, map_other, abuf, bbuf, vbuf, tbuf,
-    tcat, kcat, wcat, ycat, own_front, crm, cjm, gacc, ccat, fcat,
+    tcat, kcat, wcat, own_front, crm, cjm, gacc, ccat, fcat,
     keys0, keys1, xs0, xs1, x0, x1, sel0, sel1, o0, o1, rb0, rb1,
     psem, isem, rs_s, rs_r, dg_s, dg_r, ag_s, ag_r, c_s, c_r, y_s, y_r, x_s, x_r, k_s, k_r,
     s1_s, s1_r, s2_s, s2_r,
@@ -134,9 +139,9 @@
 
     cores = (c, 1 - c)
     sibling = at(x, y, 1 - c)
-    xpeer = {(d, e): at((x + d) % nx, y, cores[e]) for d in range(1, nx) for e in range(2)}
-    ypeer = {(d, e): at(x, (y + d) % ny, cores[e]) for d in range(1, ny) for e in range(2)}
-    zpeer = {d: {"sub": (z + d) % nz} for d in range(1, nz)}
+    xpeer = {(d, e): at((x + d) % nx, y, cores[e]) for d in far_first(nx) for e in range(2)}
+    ypeer = {(d, e): at(x, (y + d) % ny, cores[e]) for d in far_first(ny) for e in range(2)}
+    zpeer = {d: {"sub": (z + d) % nz} for d in far_first(nz)}
     peers = [sibling, *xpeer.values(), *ypeer.values(), *zpeer.values()]
     started = []
 
@@ -157,7 +162,8 @@
     for q in range(chunks):
         rows = pl.ds(q * per * width, per * width)
         loads.append(pltpu.make_async_copy(panels.at[rows], pv.at[rows], psem.at[q]))
-        loads[-1].start()
+        if q < AHEAD:
+            loads[-1].start()
         if q == 0:
             inputs = []
             small = ((coup_hbm, coup_ref), (map_hbm, map_ref), (band_hbm, band_ref), (slot_hbm, slot_ref))
@@ -167,6 +173,8 @@
     inputs[0].wait()
     for q in range(chunks):
         loads[q].wait()
+        if q + AHEAD < chunks:
+            loads[q + AHEAD].start()
         block = pv[q * per * width : (q + 1) * per * width, :]
         part = dot(block.T, block)
         gram[...] = part if q == 0 else gram[...] + part
@@ -178,17 +186,17 @@
     side, mixed, last = halves(gram[...] * (1.0 / (nz * ns)))
     gram[0:half, 0:half] = side
     gram[0:half, half:] = mixed
-    ends[pl.ds(z, 1)] = jnp.broadcast_to(last, (8, half))[None]
+    ends[pl.ds(z, 1)] = last[None]
     for copy in inputs[1:]:
         copy.wait()
     pl.semaphore_wait(barrier, len(peers))
 
-    rcopies = [
-        send(gram.at[pl.ds(((z + d) % nz) * slab, slab)], rsbuf.at[d], rs_s.at[d], rs_r.at[d], zpeer[d])
-        for d in range(1, nz)
-    ]
+    rcopies = {
+        d: send(gram.at[pl.ds(((z + d) % nz) * slab, slab)], rsbuf.at[d], rs_s.at[d], rs_r.at[d], peer)
+        for d, peer in zpeer.items()
+    }
     maps = send(map_ref, map_other, c_s.at[0], c_r.at[0], sibling)
-    dcopies = [send(ends.at[z], ends.at[z], dg_s.at[d], dg_r.at[d], zpeer[d]) for d in range(1, nz)]
+    dcopies = [send(ends.at[z], ends.at[z], dg_s.at[d], dg_r.at[d], peer) for d, peer in zpeer.items()]
     p0, p1 = c * nx + x, c * ny + y
     keys = band_ref[...] * ns + slot_ref[...]
     keys = jnp.concatenate([keys, jnp.full((8 - keys.shape[0], ns), -1, jnp.int32)], axis=0)
@@ -209,9 +217,7 @@
     even = jnp.where(c == 1, other, mine)
     identity = diagonal(width).astype(F32)
     pack_map(product(odd, even), abuf.at[y])
-    acopies = [
-        send(abuf.at[y], abuf.at[y], y_s.at[0, d], y_r.at[0, d], ypeer[d, 0]) for d in range(1, ny)
-    ]
+    acopies = [send(abuf.at[y], abuf.at[y], y_s.at[0, d], y_r.at[0, d], ypeer[d, 0]) for d in far_first(ny)]
     ch, cl = split(jnp.concatenate([crm[0], crm[1]], axis=1))
     ccat[0, :, 0:width], ccat[0, :, width : 2 * width], ccat[0, :, 2 * width :] = ch, ch, cl
     ch, cl = split(cjm[...])
@@ -219,36 +225,30 @@
     own = pl.ds(pl.multiple_of(z * slab, slab), slab)
     total = gram[own, :]
     for d in range(1, nz):
-        rcopies[d - 1].wait_recv()
+        rcopies[d].wait_recv()
         total = total + rsbuf[d]
     upd[own, :] = total
-    gcopies = [send(upd.at[own], upd.at[own], ag_s.at[d], ag_r.at[d], zpeer[d]) for d in range(1, nz)]
+    gcopies = [send(upd.at[own], upd.at[own], ag_s.at[d], ag_r.at[d], peer) for d, peer in zpeer.items()]
     for copy in dcopies:
         copy.wait_recv()
     last = ends[0]
     for m in range(1, nz):
         last = last + ends[m]
+    last = jnp.broadcast_to(last, (8, half))
     upd[half : half + 8, 0:half] = last
     upd[half : half + 8, half:] = jnp.zeros_like(last)
 
     def fill(cat, index, value):
         high, low = split(value)
-        base = index * 3 * width
-        cat[:, base : base + width] = high
-        cat[:, base + width : base + 2 * width] = high
-        cat[:, base + 2 * width : base + 3 * width] = low
-
-    def conjugate(cat, buffer, count):
-        for m in range(count):
-            high, low = split(one_sided(*unpack(buffer.at[m])))
-            base = m * 3 * width
-            value = dot(cat[:, base : base + 3 * width], jnp.concatenate([high, low, high], axis=0))
-            high, low = split(value)
-            ycat[:, base : base + width] = high
-            ycat[:, base + width : base + 2 * width] = low
-            ycat[:, base + 2 * width : base + 3 * width] = high
-        span = count * 3 * width
-        return dot_t(ycat[:, 0:span], cat[:, 0:span])
+        cat[index, :, 0:width] = high
+        cat[index, :, width : 2 * width] = high
+        cat[index, :, 2 * width :] = low
+
+    def term(cat, buffer, m):
+        high, low = split(one_sided(*unpack(buffer.at[m])))
+        spread = cat[m]
+        high, low = split(dot(spread, jnp.concatenate([high, low, high], axis=0)))
+        return dot_t(jnp.concatenate([high, low, high], axis=1), spread)
 
     for copy in gcopies:
         copy.wait_recv()
@@ -261,38 +261,42 @@
     side, mixed, last = halves_of_sum(product_t(product(odd, upd_even), odd))
     side, mixed = side + upd_odd[0:half, 0:half], mixed + upd_odd[0:half, half:]
     pack((side, mixed, last + upd_odd[half : half + 1, 0:half]), vbuf.at[y])
-    vcopies = [
-        send(vbuf.at[y], vbuf.at[y], y_s.at[1, d], y_r.at[1, d], ypeer[d, 0]) for d in range(1, ny)
-    ]
+    vcopies = {
+        d: send(vbuf.at[y], vbuf.at[y], y_s.at[1, d], y_r.at[1, d], ypeer[d, 0]) for d in far_first(ny)
+    }
     for copy in acopies:
         copy.wait_recv()
     group = [unpack_map(abuf.at[m]) for m in range(ny)]
+    fill(tcat, ny - 1, identity)
     running = group[ny - 1]
     for m in range(ny - 2, -1, -1):
         fill(tcat, m, running)
         running = product(running, group[m])
     pack_map(running, bbuf.at[x])
-    bcopies = [
-        send(bbuf.at[x], bbuf.at[x], x_s.at[0, d], x_r.at[0, d], xpeer[d, 0]) for d in range(1, nx)
-    ]
+    bcopies = [send(bbuf.at[x], bbuf.at[x], x_s.at[0, d], x_r.at[0, d], xpeer[d, 0]) for d in far_first(nx)]
     running = jnp.where(c == 1, even, identity)
     for m in range(ny - 2, -1, -1):
         fill(kcat, m, jnp.where(m < y, running, 0.0))
         running = product(running, jnp.where(m < y, group[m], identity))
     to_band = running
-
-    for copy in vcopies:
-        copy.wait_recv()
-    side, mixed, last = unpack(vbuf.at[ny - 1])
-    more_side, more_mixed, more_last = halves_of_sum(conjugate(tcat, vbuf, ny - 1))
-    pack((side + more_side, mixed + more_mixed, last + more_last), tbuf.at[x])
-    tcopies = [
-        send(tbuf.at[x], tbuf.at[x], x_s.at[1, d], x_r.at[1, d], xpeer[d, 0]) for d in range(1, nx)
-    ]
-    own_front[...] = jnp.where(c == 1, upd_even, 0.0) + conjugate(kcat, vbuf, ny - 1)
+    fill(kcat, ny - 1, jnp.zeros_like(running))
+
+    total = term(tcat, vbuf, y)
+    for d in reversed(far_first(ny)):
+        vcopies[d].wait_recv()
+        total = total + term(tcat, vbuf, (y + ny - d) % ny)
+    pack(halves_of_sum(total), tbuf.at[x])
+    tcopies = {
+        d: send(tbuf.at[x], tbuf.at[x], x_s.at[1, d], x_r.at[1, d], xpeer[d, 0]) for d in far_first(nx)
+    }
+    total = jnp.where(c == 1, upd_even, 0.0)
+    for d in range(1, ny):
+        total = total + term(kcat, vbuf, (y + ny - d) % ny)
+    own_front[...] = total
     for copy in bcopies:
         copy.wait_recv()
     running = to_band
+    fill(wcat, nx - 1, jnp.zeros_like(running))
     for m in range(nx - 2, -1, -1):
         fill(wcat, m, jnp.where(m < x, running, 0.0))
         if m:
@@ -318,9 +322,10 @@
 
     sel0[...] = selection(keys0, ny, lambda m, core: at(x, m, core))
     sel1[...] = selection(keys1, nx, lambda m, core: at(m, y, core))
-    for copy in tcopies:
-        copy.wait_recv()
-    front = own_front[...] + conjugate(wcat, tbuf, nx - 1)
+    front = own_front[...]
+    for d in reversed(far_first(nx)):
+        tcopies[d].wait_recv()
+        front = front + term(wcat, tbuf, (x + nx - d) % nx)
     front = front + front.T
     front_ref[...] = front
 
@@ -412,7 +417,7 @@
         pltpu.VMEM((listed, ns), jnp.int32),
         pltpu.VMEM((listed, ns), jnp.int32),
         pltpu.VMEM((width, width), F32),
-        pltpu.VMEM((nz, 8, half), F32),
+        pltpu.VMEM((nz, 1, half), F32),
         pltpu.VMEM((nz, half // nz, width), F32),
         pltpu.VMEM((half + 8, width), F32),
         pltpu.VMEM((half + 8, width), F32),
@@ -421,10 +426,9 @@
         pltpu.VMEM((nx, *mapmsg), BF16),
         pltpu.VMEM((ny, *symmsg), BF16),
         pltpu.VMEM((nx, *symmsg), BF16),
-        pltpu.VMEM((width, 3 * width * (ny - 1)), BF16),
-        pltpu.VMEM((width, 3 * width * (ny - 1)), BF16),
-        pltpu.VMEM((width, 3 * width * (nx - 1)), BF16),
-        pltpu.VMEM((width, 3 * width * (far - 1)), BF16),
+        pltpu.VMEM((ny, width, 3 * width), BF16),
+        pltpu.VMEM((ny, width, 3 * width), BF16),
+        pltpu.VMEM((nx, width, 3 * width), BF16),
         pltpu.VMEM((width, width), F32),
         pltpu.VMEM((2, nr * ns, half), F32),
         pltpu.VMEM((nr * ns, width), F32),

time: 58.9 us -> 57.1 us (0.969)
  Pallas kernels: 56.7 us -> 54.8 us
    pallas_call x1, Pallas kernels: 56.7 us -> 54.8 us  [body(): pl.pallas_call(functools.partial(kernel, nx, ny, nz, ns, nr), out_shape=(...]
where the time goes in v4:
time: 57.1 us; the launch traced here: 57 us
  Pallas kernels  54.8 us (96%)
  local copies, waits for them, and re-layouts  1.5 us (3%)
  between operations  0.64 us (1%)
    pallas_call x1, Pallas kernels, body(): pl.pallas_call(functools.partial(kernel, nx, ny, nz, ns, nr), out_shape=(...  54.8 us
    unnamed x2, local copies, waits for them, and re-layouts  1.5 us

profile of v4, /device:TPU:1, one launch (start us, length us, event | category | flops | bytes accessed | tf_op | source)
XLA Modules:
  0.0 57.0 jit_solution(15333452585477971289)
XLA Ops:
  0.6 54.8 %chain.1 = (f32[256,256]{1,0:T(8,128)S(1)}, f32[512,256]{1,0:T(8,128)S(1)}) custom-call(bf16[8192,256]{1,0:T(8,128)(2,1)} %bitcast.9, f32[256,256]{1,0:T(8,128)} %bitcast.10, bf16[512,256]{1,0:T(8,128)(2,1)} %bitcast.11, s32[4,32]{1,0:T(4,128)} %bitcast.12, s32[4,32]{1,0:T(4,128)} %bitcast.13), custom_call_target="tpu_custom_call" | custom-call | tf_op jit(solution)/shard_map/chain/pallas_call | solution.py:459
  55.5 0.7 %copy.9 = f32[1,256,256]{2,1,0:T(8,128)} copy(f32[1,256,256]{2,1,0:T(8,128)S(1)} %bitcast.8) | data formatting | bytes 524288
  56.2 0.8 %copy.10 = f32[1,1,32,16,256]{4,3,2,1,0:T(8,128)} copy(f32[1,1,32,16,256]{4,3,2,1,0:T(8,128)S(1)} %bitcast.7) | data formatting | bytes 1048576

commit v5 on v4

--- a/solution.py
+++ b/solution.py
@@ -90,6 +90,12 @@
     low = jnp.where(rows > cols, mixed, jnp.where(middle, 0.5 * last, 0.0))
     top = jnp.concatenate([first, side], axis=1)
     return jnp.concatenate([top, jnp.concatenate([jnp.zeros_like(side), low], axis=1)], axis=0)
+
+
+def parts_of(rows):
+    half = rows.shape[1] // 2
+    mixed = jnp.where(diagonal(half), rows[half : half + 1, 0:half], rows[0:half, half:])
+    return rows[0:half, 0:half], mixed, rows[half : half + 1, half:]
 
 
 def pack(parts, message):
@@ -122,7 +128,7 @@
     nx, ny, nz, ns, nr,
     panels, map_hbm, coup_hbm, band_hbm, slot_hbm,
     front_ref, grads_ref,
-    pv, map_ref, coup_ref, band_ref, slot_ref, gram, ends, rsbuf, upd, upd_other, map_other, abuf, bbuf, vbuf, tbuf,
+    pv, map_ref, coup_ref, band_ref, slot_ref, gram, shares, ends, rsbuf, upd, upd_other, map_other, abuf, bbuf, vbuf, tbuf,
     tcat, kcat, wcat, own_front, crm, cjm, gacc, ccat, fcat,
     keys0, keys1, xs0, xs1, x0, x1, sel0, sel1, o0, o1, rb0, rb1,
     psem, isem, rs_s, rs_r, dg_s, dg_r, ag_s, ag_r, c_s, c_r, y_s, y_r, x_s, x_r, k_s, k_r,
@@ -142,7 +148,7 @@
     xpeer = {(d, e): at((x + d) % nx, y, cores[e]) for d in far_first(nx) for e in range(2)}
     ypeer = {(d, e): at(x, (y + d) % ny, cores[e]) for d in far_first(ny) for e in range(2)}
     zpeer = {d: {"sub": (z + d) % nz} for d in far_first(nz)}
-    peers = [sibling, *xpeer.values(), *ypeer.values(), *zpeer.values()]
+    peers = [*zpeer.values(), *xpeer.values(), *ypeer.values(), sibling]
     started = []
 
     def send(src, dst, s, r, target):
@@ -184,15 +190,16 @@
             for h in range(2):
                 crm[h, pl.ds(j, nr, stride=ns), :] = value[:, h * half : (h + 1) * half]
     side, mixed, last = halves(gram[...] * (1.0 / (nz * ns)))
-    gram[0:half, 0:half] = side
-    gram[0:half, half:] = mixed
-    ends[pl.ds(z, 1)] = last[None]
+    packed = jnp.concatenate([side, mixed], axis=1)
+    gram[0:half, :] = packed
+    shares[...] = packed.astype(BF16)
+    ends[pl.ds(z, 1)] = jnp.concatenate([pick(mixed), last], axis=1)[None]
     for copy in inputs[1:]:
         copy.wait()
     pl.semaphore_wait(barrier, len(peers))
 
     rcopies = {
-        d: send(gram.at[pl.ds(((z + d) % nz) * slab, slab)], rsbuf.at[d], rs_s.at[d], rs_r.at[d], peer)
+        d: send(shares.at[pl.ds(((z + d) % nz) * slab, slab)], rsbuf.at[d], rs_s.at[d], rs_r.at[d], peer)
         for d, peer in zpeer.items()
     }
     maps = send(map_ref, map_other, c_s.at[0], c_r.at[0], sibling)
@@ -226,7 +233,7 @@
     total = gram[own, :]
     for d in range(1, nz):
         rcopies[d].wait_recv()
-        total = total + rsbuf[d]
+        total = total + rsbuf[d].astype(F32)
     upd[own, :] = total
     gcopies = [send(upd.at[own], upd.at[own], ag_s.at[d], ag_r.at[d], peer) for d, peer in zpeer.items()]
     for copy in dcopies:
@@ -234,9 +241,7 @@
     last = ends[0]
     for m in range(1, nz):
         last = last + ends[m]
-    last = jnp.broadcast_to(last, (8, half))
-    upd[half : half + 8, 0:half] = last
-    upd[half : half + 8, half:] = jnp.zeros_like(last)
+    upd[half : half + 8, :] = jnp.broadcast_to(last, (8, width))
 
     def fill(cat, index, value):
         high, low = split(value)
@@ -257,10 +262,10 @@
     mine, other = upd[...], upd_other[...]
     upd_odd = jnp.where(c == 1, mine, other)
     upd_even = jnp.where(c == 1, other, mine)
-    upd_even = one_sided(upd_even[0:half, 0:half], upd_even[0:half, half:], upd_even[half : half + 1, 0:half])
+    upd_even = one_sided(*parts_of(upd_even))
     side, mixed, last = halves_of_sum(product_t(product(odd, upd_even), odd))
-    side, mixed = side + upd_odd[0:half, 0:half], mixed + upd_odd[0:half, half:]
-    pack((side, mixed, last + upd_odd[half : half + 1, 0:half]), vbuf.at[y])
+    more = parts_of(upd_odd)
+    pack((side + more[0], mixed + more[1], last + more[2]), vbuf.at[y])
     vcopies = {
         d: send(vbuf.at[y], vbuf.at[y], y_s.at[1, d], y_r.at[1, d], ypeer[d, 0]) for d in far_first(ny)
     }
@@ -323,8 +328,9 @@
     sel0[...] = selection(keys0, ny, lambda m, core: at(x, m, core))
     sel1[...] = selection(keys1, nx, lambda m, core: at(m, y, core))
     front = own_front[...]
-    for d in reversed(far_first(nx)):
-        tcopies[d].wait_recv()
+    for copy in tcopies.values():
+        copy.wait_recv()
+    for d in range(1, nx):
         front = front + term(wcat, tbuf, (x + nx - d) % nx)
     front = front + front.T
     front_ref[...] = front
@@ -362,7 +368,7 @@
     adjoint = dot(ccat[1], fcat[...])
     for h in range(2):
         gacc[h] = adjoint[:, h * half : (h + 1) * half]
-    scatters = []
+    scatters = {}
     for q in range(CHUNKS):
         for h, sel, xx, oo, rb, count, all_peers in (
             (0, sel0, x0, o0, rb0, ny, ypeer), (1, sel1, x1, o1, rb1, nx, xpeer),
@@ -374,27 +380,30 @@
                 span = slice(first, first + width)
                 oo[:, span] = dot(sel[...], xx[:, span]).astype(BF16)
             span = pl.ds(q * piece, piece)
+            scatters[q, h] = []
             for (d, e), peer in {**all_peers, (0, 1): sibling}.items():
                 rows = pl.ds(pl.multiple_of((cores[e] * count + (here + d) % count) * ns, ns), ns)
-                scatters.append(
+                scatters[q, h].append(
                     send(
                         oo.at[rows, span], rb.at[d, e, :, span],
                         s2_s.at[q, h, d, e], s2_r.at[q, h, d, e], peer,
                     )
                 )
-    for copy in scatters:
-        copy.wait_recv()
-    for h, oo, rb, count, here in ((0, o0, rb0, ny, y), (1, o1, rb1, nx, x)):
-        rows = pl.ds(pl.multiple_of((c * count + here) * ns, ns), ns)
-        same, cross = oo[rows, :].astype(F32), rb[0, 1].astype(F32)
-        for d in range(1, count):
-            same, cross = same + rb[d, 0].astype(F32), cross + rb[d, 1].astype(F32)
-        parts = jnp.where(c == 0, same, cross), jnp.where(c == 0, cross, same)
-        for r in range(nr):
-            place = (h, pl.ds(r, ns, stride=nr), slice(None))
-            lane = r % (nr // 2) * half
-            gacc[place] = gacc[place] + parts[r // (nr // 2)][:, lane : lane + half]
-        grads_ref[:, h * half : (h + 1) * half] = gacc[h]
+    for q in range(CHUNKS):
+        for h, oo, rb, count, here in ((0, o0, rb0, ny, y), (1, o1, rb1, nx, x)):
+            for copy in scatters[q, h]:
+                copy.wait_recv()
+            span = pl.ds(q * piece, piece)
+            rows = pl.ds(pl.multiple_of((c * count + here) * ns, ns), ns)
+            same, cross = oo[rows, span].astype(F32), rb[0, 1, :, span].astype(F32)
+            for d in range(1, count):
+                same, cross = same + rb[d, 0, :, span].astype(F32), cross + rb[d, 1, :, span].astype(F32)
+            for core, part in enumerate((jnp.where(c == 0, same, cross), jnp.where(c == 0, cross, same))):
+                for r in range(piece // half):
+                    place = (h, pl.ds((core * CHUNKS + q) * (piece // half) + r, ns, stride=nr), slice(None))
+                    gacc[place] = gacc[place] + part[:, r * half : (r + 1) * half]
+            if q == CHUNKS - 1:
+                grads_ref[:, h * half : (h + 1) * half] = gacc[h]
     for copy in started:
         copy.wait_send()
 
@@ -417,8 +426,9 @@
         pltpu.VMEM((listed, ns), jnp.int32),
         pltpu.VMEM((listed, ns), jnp.int32),
         pltpu.VMEM((width, width), F32),
-        pltpu.VMEM((nz, 1, half), F32),
-        pltpu.VMEM((nz, half // nz, width), F32),
+        pltpu.VMEM((half, width), BF16),
+        pltpu.VMEM((nz, 1, width), F32),
+        pltpu.VMEM((nz, half // nz, width), BF16),
         pltpu.VMEM((half + 8, width), F32),
         pltpu.VMEM((half + 8, width), F32),
         pltpu.VMEM((width, width), F32),

time: 57.1 us -> 55.2 us (0.967)
  Pallas kernels: 54.8 us -> 52.9 us
    pallas_call x1, Pallas kernels: 54.8 us -> 52.9 us  [body(): pl.pallas_call(functools.partial(kernel, nx, ny, nz, ns, nr), out_shape=(...]
where the time goes in v5:
time: 55.2 us; the launch traced here: 55 us
  Pallas kernels  52.9 us (96%)
  local copies, waits for them, and re-layouts  1.5 us (3%)
  between operations  0.64 us (1%)
    pallas_call x1, Pallas kernels, body(): pl.pallas_call(functools.partial(kernel, nx, ny, nz, ns, nr), out_shape=(...  52.9 us
    unnamed x2, local copies, waits for them, and re-layouts  1.5 us

profile of v5, /device:TPU:1, one launch (start us, length us, event | category | flops | bytes accessed | tf_op | source)
XLA Modules:
  0.0 55.0 jit_solution(10728858494336451747)
XLA Ops:
  0.6 52.9 %chain.1 = (f32[256,256]{1,0:T(8,128)S(1)}, f32[512,256]{1,0:T(8,128)S(1)}) custom-call(bf16[8192,256]{1,0:T(8,128)(2,1)} %bitcast.9, f32[256,256]{1,0:T(8,128)} %bitcast.10, bf16[512,256]{1,0:T(8,128)(2,1)} %bitcast.11, s32[4,32]{1,0:T(4,128)} %bitcast.12, s32[4,32]{1,0:T(4,128)} %bitcast.13), custom_call_target="tpu_custom_call" | custom-call | tf_op jit(solution)/shard_map/chain/pallas_call | solution.py:469
  53.5 0.7 %copy.9 = f32[1,256,256]{2,1,0:T(8,128)} copy(f32[1,256,256]{2,1,0:T(8,128)S(1)} %bitcast.8) | data formatting | bytes 524288
  54.2 0.8 %copy.10 = f32[1,1,32,16,256]{4,3,2,1,0:T(8,128)} copy(f32[1,1,32,16,256]{4,3,2,1,0:T(8,128)S(1)} %bitcast.7) | data formatting | bytes 1048576

commit v6 on v5

--- a/solution.py
+++ b/solution.py
@@ -249,8 +249,9 @@
         cat[index, :, width : 2 * width] = high
         cat[index, :, 2 * width :] = low
 
-    def term(cat, buffer, m):
-        high, low = split(one_sided(*unpack(buffer.at[m])))
+    def term(cat, buffer, m, there=None):
+        matrix = one_sided(*unpack(buffer.at[m]))
+        high, low = split(matrix if there is None else jnp.where(there, matrix, 0.0))
         spread = cat[m]
         high, low = split(dot(spread, jnp.concatenate([high, low, high], axis=0)))
         return dot_t(jnp.concatenate([high, low, high], axis=1), spread)
@@ -278,7 +279,15 @@
         fill(tcat, m, running)
         running = product(running, group[m])
     pack_map(running, bbuf.at[x])
-    bcopies = [send(bbuf.at[x], bbuf.at[x], x_s.at[0, d], x_r.at[0, d], xpeer[d, 0]) for d in far_first(nx)]
+    bcopies = {
+        d: pltpu.make_async_remote_copy(
+            src_ref=bbuf.at[x], dst_ref=bbuf.at[x], send_sem=x_s.at[0, d], recv_sem=x_r.at[0, d],
+            device_id=xpeer[d, 0], device_id_type=MESH,
+        )
+        for d in far_first(nx)
+    }
+    for d, copy in bcopies.items():
+        pl.when((x >= 1) & (x + d < nx))(copy.start)
     running = jnp.where(c == 1, even, identity)
     for m in range(ny - 2, -1, -1):
         fill(kcat, m, jnp.where(m < y, running, 0.0))
@@ -292,14 +301,20 @@
         total = total + term(tcat, vbuf, (y + ny - d) % ny)
     pack(halves_of_sum(total), tbuf.at[x])
     tcopies = {
-        d: send(tbuf.at[x], tbuf.at[x], x_s.at[1, d], x_r.at[1, d], xpeer[d, 0]) for d in far_first(nx)
+        d: pltpu.make_async_remote_copy(
+            src_ref=tbuf.at[x], dst_ref=tbuf.at[x], send_sem=x_s.at[1, d], recv_sem=x_r.at[1, d],
+            device_id=xpeer[d, 0], device_id_type=MESH,
+        )
+        for d in far_first(nx)
     }
+    for d, copy in tcopies.items():
+        pl.when(x + d < nx)(copy.start)
     total = jnp.where(c == 1, upd_even, 0.0)
     for d in range(1, ny):
         total = total + term(kcat, vbuf, (y + ny - d) % ny)
     own_front[...] = total
-    for copy in bcopies:
-        copy.wait_recv()
+    for d, copy in bcopies.items():
+        pl.when(x >= d + 1)(copy.wait_recv)
     running = to_band
     fill(wcat, nx - 1, jnp.zeros_like(running))
     for m in range(nx - 2, -1, -1):
@@ -328,10 +343,10 @@
     sel0[...] = selection(keys0, ny, lambda m, core: at(x, m, core))
     sel1[...] = selection(keys1, nx, lambda m, core: at(m, y, core))
     front = own_front[...]
-    for copy in tcopies.values():
-        copy.wait_recv()
+    for d, copy in tcopies.items():
+        pl.when(x >= d)(copy.wait_recv)
     for d in range(1, nx):
-        front = front + term(wcat, tbuf, (x + nx - d) % nx)
+        front = front + term(wcat, tbuf, (x + nx - d) % nx, x >= d)
     front = front + front.T
     front_ref[...] = front
 
@@ -406,6 +421,9 @@
                 grads_ref[:, h * half : (h + 1) * half] = gacc[h]
     for copy in started:
         copy.wait_send()
+    for d in far_first(nx):
+        pl.when(x + d < nx)(tcopies[d].wait_send)
+        pl.when((x >= 1) & (x + d < nx))(bcopies[d].wait_send)
 
 
 def body(nx, ny, panels, chain_map, couplers, anc_band, anc_slot):

time: 55.2 us -> 54.1 us (0.980)
  Pallas kernels: 52.9 us -> 51.8 us
    pallas_call x1, Pallas kernels: 52.9 us -> 51.8 us  [body(): pl.pallas_call(functools.partial(kernel, nx, ny, nz, ns, nr), out_shape=(...]
where the time goes in v6:
time: 54.1 us; the launch traced here: 53.9 us
  Pallas kernels  51.8 us (96%)
  local copies, waits for them, and re-layouts  1.5 us (3%)
  between operations  0.64 us (1%)
    pallas_call x1, Pallas kernels, body(): pl.pallas_call(functools.partial(kernel, nx, ny, nz, ns, nr), out_shape=(...  51.8 us
    unnamed x2, local copies, waits for them, and re-layouts  1.5 us

profile of v6, /device:TPU:1, one launch (start us, length us, event | category | flops | bytes accessed | tf_op | source)
XLA Modules:
  0.0 53.9 jit_solution(12434128749674905773)
XLA Ops:
  0.6 51.8 %chain.1 = (f32[256,256]{1,0:T(8,128)S(1)}, f32[512,256]{1,0:T(8,128)S(1)}) custom-call(bf16[8192,256]{1,0:T(8,128)(2,1)} %bitcast.9, f32[256,256]{1,0:T(8,128)} %bitcast.10, bf16[512,256]{1,0:T(8,128)(2,1)} %bitcast.11, s32[4,32]{1,0:T(4,128)} %bitcast.12, s32[4,32]{1,0:T(4,128)} %bitcast.13), custom_call_target="tpu_custom_call" | custom-call | tf_op jit(solution)/shard_map/chain/pallas_call | solution.py:487
  52.4 0.7 %copy.9 = f32[1,256,256]{2,1,0:T(8,128)} copy(f32[1,256,256]{2,1,0:T(8,128)S(1)} %bitcast.8) | data formatting | bytes 524288
  53.1 0.8 %copy.10 = f32[1,1,32,16,256]{4,3,2,1,0:T(8,128)} copy(f32[1,1,32,16,256]{4,3,2,1,0:T(8,128)S(1)} %bitcast.7) | data formatting | bytes 1048576

commit v7 on v6

--- a/solution.py
+++ b/solution.py
@@ -184,11 +184,6 @@
         block = pv[q * per * width : (q + 1) * per * width, :]
         part = dot(block.T, block)
         gram[...] = part if q == 0 else gram[...] + part
-        for j in range(q * per, (q + 1) * per):
-            value = dot(coup_ref[j * nr : (j + 1) * nr, :], pv[j * width : (j + 1) * width, :])
-            cjm[j * nr : (j + 1) * nr, :] = value
-            for h in range(2):
-                crm[h, pl.ds(j, nr, stride=ns), :] = value[:, h * half : (h + 1) * half]
     side, mixed, last = halves(gram[...] * (1.0 / (nz * ns)))
     packed = jnp.concatenate([side, mixed], axis=1)
     gram[0:half, :] = packed
@@ -218,6 +213,11 @@
     kcopies.append(send(own, own, k_s.at[1, 0, 1], k_r.at[1, 0, 1], sibling))
     for (d, e), peer in ypeer.items():
         kcopies.append(send(own, own, k_s.at[1, d, e], k_r.at[1, d, e], peer))
+    for j in range(ns):
+        value = dot(coup_ref[j * nr : (j + 1) * nr, :], pv[j * width : (j + 1) * width, :])
+        cjm[j * nr : (j + 1) * nr, :] = value
+        for h in range(2):
+            crm[h, pl.ds(j, nr, stride=ns), :] = value[:, h * half : (h + 1) * half]
     maps.wait_recv()
     mine, other = map_ref[...], map_other[...]
     odd = jnp.where(c == 1, mine, other)
@@ -296,8 +296,9 @@
     fill(kcat, ny - 1, jnp.zeros_like(running))
 
     total = term(tcat, vbuf, y)
-    for d in reversed(far_first(ny)):
-        vcopies[d].wait_recv()
+    for copy in vcopies.values():
+        copy.wait_recv()
+    for d in range(1, ny):
         total = total + term(tcat, vbuf, (y + ny - d) % ny)
     pack(halves_of_sum(total), tbuf.at[x])
     tcopies = {

time: 54.1 us -> 54.1 us (level)
  no operation moved by 1% of the time
where the time goes in v7:
time: 54.1 us; the launch traced here: 54 us
  Pallas kernels  51.8 us (96%)
  local copies, waits for them, and re-layouts  1.5 us (3%)
  between operations  0.64 us (1%)
    pallas_call x1, Pallas kernels, body(): pl.pallas_call(functools.partial(kernel, nx, ny, nz, ns, nr), out_shape=(...  51.8 us
    unnamed x2, local copies, waits for them, and re-layouts  1.5 us

profile of v7, /device:TPU:1, one launch (start us, length us, event | category | flops | bytes accessed | tf_op | source)
XLA Modules:
  0.0 54.0 jit_solution(5447763976979633985)
XLA Ops:
  0.6 51.8 %chain.1 = (f32[256,256]{1,0:T(8,128)S(1)}, f32[512,256]{1,0:T(8,128)S(1)}) custom-call(bf16[8192,256]{1,0:T(8,128)(2,1)} %bitcast.9, f32[256,256]{1,0:T(8,128)} %bitcast.10, bf16[512,256]{1,0:T(8,128)(2,1)} %bitcast.11, s32[4,32]{1,0:T(4,128)} %bitcast.12, s32[4,32]{1,0:T(4,128)} %bitcast.13), custom_call_target="tpu_custom_call" | custom-call | tf_op jit(solution)/shard_map/chain/pallas_call | solution.py:488
  52.5 0.7 %copy.9 = f32[1,256,256]{2,1,0:T(8,128)} copy(f32[1,256,256]{2,1,0:T(8,128)S(1)} %bitcast.8) | data formatting | bytes 524288
  53.2 0.8 %copy.10 = f32[1,1,32,16,256]{4,3,2,1,0:T(8,128)} copy(f32[1,1,32,16,256]{4,3,2,1,0:T(8,128)S(1)} %bitcast.7) | data formatting | bytes 1048576
